TPU v7x, 128 devices: a whole 4x4x4 slice. The times are simulated.
128 devices in a mesh: row: 16 (over z, x_hi, core), col: 8 (over y, x_lo).
Axes of the slice: x: 4 (x_hi: 2, x_lo: 2; x = x_hi * 2 + x_lo), y: 4, z: 4, core: 2. Of those that a mesh axis runs over, the one named last changes fastest.
Arguments:
- blocks: bfloat16 [512, 16, 128, 128], P('row', 'col'), may hold values from -0.8984375 to 0.8984375
- pattern: int32 [512, 16], replicated, may hold values from 0 to 511, as said below
- anchors: int32 [3, 512, 16], replicated, may hold values from 0 to 255, as said below
- basis_x: bfloat16 [16, 128], replicated, may hold values from -0.5 to 0.5
- basis_yz: bfloat16 [128, 256], replicated, may hold values from -0.5 to 0.5
Outputs:
- square: float32 [512, 16, 128, 128], P('row', 'col')
- grid_values: float32 [256, 128, 128], P('row', 'col')
Inputs may be any that keep to these rules, and one draw needn't show every extreme that they name: pattern[i,k] = (i + d) mod 512 with -8 <= d <= 8; the 16 columns of a row are distinct. For block row i in group g = i // 32, anchors[0,i,k] = (g * 16 - 16 / 2 + u) mod 256 with 0 <= u <= 16; anchors[1,i,k] <= 112; anchors[2,i,k] <= 112.
All inputs are finite; a program needn't handle non-finite values.
Results may differ from a plain program's by a relative error of at most 0.0041.
Values may be sent and summed in bfloat16 or wider, within the bound.
A program may use at most 128 MiB of HBM per device.

v0:
```python
import math

import jax
import jax.numpy as jnp
from jax import lax
from jax.sharding import PartitionSpec as P

H = 8
PL = 16
GY = 128
GZ = 128
TX = 16
TY = 16
TZ = 16


def from_behind(value, axis, by):
    peers = lax.axis_size(axis)
    return lax.ppermute(value, axis, [(i, (i + by) % peers) for i in range(peers)])


def extended_2(cells, sides, width):
    for axis, dim in sides:
        count = lax.axis_size(axis)
        head = lax.slice_in_dim(cells, 0, width, axis=dim)
        tail = lax.slice_in_dim(cells, cells.shape[dim] - width, cells.shape[dim], axis=dim)
        cells = jnp.concatenate(
            [
                lax.ppermute(tail, axis, [(i, (i + 1) % count) for i in range(count)]),
                cells,
                lax.ppermute(head, axis, [((i + 1) % count, i) for i in range(count)]),
            ],
            axis=dim,
        )
    return cells


def fold_rims(slab, margin):
    upper_rim = slab[slab.shape[0] - margin :]
    lower_rim = slab[:margin]
    from_below = from_behind(upper_rim, "row", 1)
    from_above = from_behind(lower_rim, "row", -1)
    interior = slab[margin : slab.shape[0] - margin]
    interior = interior.at[:margin].add(from_below)
    interior = interior.at[interior.shape[0] - margin :].add(from_above)
    return interior


def share_sums(slab):
    return lax.psum_scatter(slab, "col", scatter_dimension=1, tiled=True)


def per_device(blocks, pattern, anchors, basis_x, basis_yz):
    rows_dev, slots, bsize, _ = blocks.shape
    kslots = pattern.shape[1]
    row_count = lax.axis_size("row")
    row_place = lax.axis_index("row")
    col_place = lax.axis_index("col")
    total_rows = rows_dev * row_count
    full_rows = lax.all_gather(blocks, "col", axis=1, tiled=True)
    extended = extended_2(full_rows, (("row", 0),), H)
    span_rows = rows_dev + 2 * H
    stacked = jnp.concatenate(
        [
            extended.reshape(span_rows * kslots, bsize, bsize),
            jnp.zeros((1, bsize, bsize), jnp.bfloat16),
        ],
        axis=0,
    )
    first_row = row_place * rows_dev
    own_pattern = lax.dynamic_slice_in_dim(pattern, first_row, rows_dev, 0)
    own_targets = lax.dynamic_slice_in_dim(own_pattern, col_place * slots, slots, 1)
    slot_ids = jnp.arange(kslots, dtype=jnp.int32)

    def one_row(row_local):
        columns = own_pattern[row_local]
        targets = own_targets[row_local]
        far_pattern = pattern[columns]
        matches = (far_pattern[:, :, None] == targets[None, None, :]).astype(jnp.int32)
        matched = jnp.sum(matches, axis=1)
        match_slot = jnp.sum(matches * slot_ids[None, :, None], axis=1)
        local_row = (columns - first_row + H) % total_rows
        block_index = jnp.where(
            matched > 0, local_row[:, None] * kslots + match_slot, span_rows * kslots
        )
        picked = stacked[block_index]
        left_blocks = lax.dynamic_index_in_dim(extended, row_local + H, 0, keepdims=False)
        return jnp.einsum("kmn,ksnp->smp", left_blocks, picked, preferred_element_type=jnp.float32)

    square = lax.map(one_row, jnp.arange(rows_dev, dtype=jnp.int32))
    density = square.astype(jnp.bfloat16)
    task_count = rows_dev * slots
    density_rows = density.reshape(task_count, bsize, bsize)
    halves = jnp.einsum(
        "am,qmn->qan", basis_x, density_rows, preferred_element_type=jnp.float32
    ).astype(jnp.bfloat16)
    tile_values = jnp.einsum(
        "qan,nc->qac", halves, basis_yz, preferred_element_type=jnp.float32
    ).reshape(task_count, TX, TY, TZ)
    own_anchors = lax.dynamic_slice(
        anchors, (0, first_row, col_place * slots), (3, rows_dev, slots)
    ).reshape(3, task_count)
    margin = TX // 2
    grid_planes = PL * row_count
    slab_planes = PL + 2 * margin
    first_cells = (own_anchors[0] - row_place * PL + margin) % grid_planes
    grid_y = GY
    grid_z = GZ
    batch_size = math.gcd(task_count, 8)
    batch_count = task_count // batch_size
    tile_batches = tile_values.reshape(batch_count, batch_size, TX, TY, TZ)
    plane_starts = first_cells.reshape(batch_count, batch_size)
    row_starts = own_anchors[1].reshape(batch_count, batch_size)
    cell_starts = own_anchors[2].reshape(batch_count, batch_size)
    highest = lax.Precision.HIGHEST

    def place_batch(slab, inputs):
        tiles, plane_first, row_first, cell_first = inputs
        plane_cells = plane_first[:, None] + jnp.arange(TX, dtype=jnp.int32)[None, :]
        plane_pick = (
            plane_cells[:, :, None] == jnp.arange(slab_planes, dtype=jnp.int32)[None, None, :]
        ).astype(jnp.float32)
        row_cells = row_first[:, None] + jnp.arange(TY, dtype=jnp.int32)[None, :]
        row_pick = (
            row_cells[:, :, None] == jnp.arange(grid_y, dtype=jnp.int32)[None, None, :]
        ).astype(jnp.float32)
        depth_cells = cell_first[:, None] + jnp.arange(TZ, dtype=jnp.int32)[None, :]
        cell_pick = (
            depth_cells[:, :, None] == jnp.arange(grid_z, dtype=jnp.int32)[None, None, :]
        ).astype(jnp.float32)
        placed_z = jnp.einsum("qabc,qcz->qabz", tiles, cell_pick, precision=highest)
        placed_y = jnp.einsum("qby,qabz->qayz", row_pick, placed_z, precision=highest)
        return (slab + jnp.einsum("qap,qayz->pyz", plane_pick, placed_y, precision=highest), None)

    partial_grid, _ = lax.scan(
        place_batch,
        jnp.zeros((slab_planes, grid_y, grid_z), jnp.float32),
        (tile_batches, plane_starts, row_starts, cell_starts),
    )
    grid_values = share_sums(fold_rims(partial_grid, margin))
    return (square, grid_values)


def solution(mesh):
    placed = (P("row", "col", None, None), P(), P(), P(), P())
    return jax.shard_map(
        per_device,
        mesh=mesh,
        in_specs=placed,
        out_specs=(P("row", "col", None, None), P("row", "col", None)),
        check_vma=False,
    )
```

profile of v0, /device:TPU:1, one launch (start us, length us, event | category | flops | bytes accessed | tf_op | source)
XLA Modules:
  0.0 1260.8 jit_solution(6754802180002021813)
XLA Ops:
  8.0 330.5 %all-gather.2.cloned.1.call-done = bf16[32,16,128,128]{3,2,1,0:T(8,128)(2,1)} async-done(((bf16[32,2,128,128]{3,2,1,0:T(8,128)(2,1)}), bf16[32,16,128,128]{3,2,1,0:T(8,128)(2,1)}) %all-gather.2.cloned.1.call-update) | async-done | bytes 16777232 | tf_op jit(solution)/shard_map/all_gather | solution.py:60
  338.5 6.2 fusion.37
  349.2 85.9 %collective-permute-done = bf16[8,16,128,128]{3,2,1,0:T(8,128)(2,1)} collective-permute-done((bf16[8,16,128,128]{3,2,1,0:T(8,128)(2,1)}, bf16[8,16,128,128]{3,2,1,0:T(8,128)(2,1)}, u32[]{:S(2)}, u32[]{:S(2)}) %collective-permute-start) | collective-permute-done | bytes 4194336 | tf_op jit(solution)/shard_map/ppermute | solution.py:29
  437.5 9.0 constant_dynamic-update-slice_fusion.1
  449.6 16.8 %concatenate.11 = bf16[769,128,128]{2,1,0:T(8,128)(2,1)} pad(bf16[768,128,128]{2,1,0:T(8,128)(2,1)S(1)} %bitcast.121, bf16[]{:T(256)} %constant.189.clone.1), padding=0_1x0_0x0_0 | pad | bytes 50364416 | tf_op jit(solution)/shard_map/concatenate | solution.py:63
  466.4 511.2 %while.26 = (s32[]{:T(128)}, f32[32,2,128,128]{2,3,1,0:T(8,128)}, s32[32]{0:T(128)S(1)}, s32[32,16]{1,0:T(8,128)S(1)}, s32[512,16]{1,0:T(8,128)S(1)}, /*index=5*...) while((s32[]{:T(128)}, f32[32,2,128,128]{2,3,1,0:T(8,128)}, ...), condition=%wide.region_3.4_spmd.clone, body=%wide.region_0.3_spmd.clone.sunk | while | flops 134222752 | bytes 3814989 | solution.py:90
  470.0 8.9 gather_fusion.1
  486.0 8.9 gather_fusion.1
  502.0 8.9 gather_fusion.1
  517.9 8.9 gather_fusion.1
  533.9 8.9 gather_fusion.1
  549.9 8.9 gather_fusion.1
  565.9 8.9 gather_fusion.1
  581.9 8.9 gather_fusion.1
  597.8 8.9 gather_fusion.1
  613.8 8.9 gather_fusion.1
  629.8 8.9 gather_fusion.1
  645.8 8.9 gather_fusion.1
  661.7 8.9 gather_fusion.1
  677.7 8.9 gather_fusion.1
  693.7 8.9 gather_fusion.1
  709.6 8.9 gather_fusion.1
  725.6 8.9 gather_fusion.1
  741.6 8.9 gather_fusion.1
  757.6 8.9 gather_fusion.1
  773.6 8.9 gather_fusion.1
  789.5 8.9 gather_fusion.1
  805.5 8.9 gather_fusion.1
  821.5 8.9 gather_fusion.1
  837.5 8.9 gather_fusion.1
  853.4 8.9 gather_fusion.1
  869.4 8.9 gather_fusion.1
  885.4 8.9 gather_fusion.1
  901.3 8.9 gather_fusion.1
  917.3 8.9 gather_fusion.1
  933.3 8.9 gather_fusion.1
  949.3 8.9 gather_fusion.1
  965.3 8.9 gather_fusion.1
  988.6 206.9 %while.27 = (s32[]{:T(128)}, f32[32,128,128]{2,0,1:T(8,128)S(1)}, s32[8,8]{1,0:T(8,128)S(1)}, f32[8,8,16,16,16]{4,3,2,1,0:T(8,128)}, s32[8,8]{1,0:T(8,128)S(1)}, /*index=5*/s32[8,8]{1,0:T(8,128)S(1)}, s32[]{:T(128)}, s32[]{:T(128)}) while((s32[]{:T(128)}, f32[32,128,128]{2,0,1:T(8,128)S(1)}, s32[8,8]{1,0:T(8,128)S(1)}, ...), condition=%wide.region_5.6_spmd.clone, body=%wide.region_4.5_spmd.clone.sunk | while | flops 1259377024 | bytes 40898436 | solution.py:135
  990.7 8.9 convolution_bitcast_fusion.3
  999.6 9.2 copy.57
  1008.8 5.6 bitcast_add_fusion.3
  1016.6 8.9 convolution_bitcast_fusion.3
  1025.4 9.2 copy.57
  1034.7 5.6 bitcast_add_fusion.3
  1042.4 8.9 convolution_bitcast_fusion.3
  1051.3 9.2 copy.57
  1060.6 5.6 bitcast_add_fusion.3
  1068.3 8.9 convolution_bitcast_fusion.3
  1077.2 9.2 copy.57
  1094.2 8.9 convolution_bitcast_fusion.3
  1103.1 9.2 copy.57
  1112.3 5.6 bitcast_add_fusion.3
  1120.0 8.9 convolution_bitcast_fusion.3
  1128.9 9.2 copy.57
  1145.9 8.9 convolution_bitcast_fusion.3
  1154.8 9.2 copy.57
  1171.8 8.9 convolution_bitcast_fusion.3
  1180.7 9.2 copy.57
  1189.9 5.6 bitcast_add_fusion.3
  1201.0 6.0 collective-permute-done.2
  1207.2 9.3 collective-permute-done.3
  1217.6 5.6 copy.47
  1223.3 30.7 %reduce-scatter.2.cloned.1.call-done = f32[16,16,128]{2,1,0:T(8,128)} async-done(((f32[16,128,128]{2,1,0:T(8,128)}), f32[16,16,128]{2,1,0:T(8,128)}) %reduce-scatter.2.cloned.1.call-update) | async-done | bytes 131088 | tf_op jit(solution)/shard_map/reduce_scatter | solution.py:50
  (480 shorter events, 182.6 us)
Async XLA Ops:
  7.2 974.4 %copy-start = (bf16[128,256]{1,0:T(8,128)(2,1)S(1)}, bf16[128,256]{1,0:T(8,128)(2,1)}, u32[]{:S(2)}) copy-start(bf16[128,256]{1,0:T(8,128)(2,1)} %param.17) | copy-start | bytes 196612
  7.2 331.3 %all-gather.2.cloned.1.call-start = ((), (), s32[]{:S(2)}) async-start(), calls=%async_computation.1 | async-start | bytes 18874368 | tf_op jit(solution)/shard_map/all_gather | solution.py:60
  7.9 339.7 %copy-start.4 = (s32[512,16]{0,1:T(8,128)S(1)}, s32[512,16]{0,1:T(8,128)}, u32[]{:S(2)}) copy-start(s32[512,16]{0,1:T(8,128)} %param.14) | copy-start | bytes 98308
  7.9 1246.1 %reduce-scatter.2.cloned.1.call-start = ((), (), s32[]{:S(2)}) async-start(), calls=%async_computation.2 | async-start | bytes 1179648 | tf_op jit(solution)/shard_map/reduce_scatter | solution.py:50
  344.7 90.4 %collective-permute-start = (bf16[8,16,128,128]{3,2,1,0:T(8,128)(2,1)}, bf16[8,16,128,128]{3,2,1,0:T(8,128)(2,1)}, u32[]{:S(2)}, u32[]{:S(2)}) collective-permute-start(bf16[8,16,128,128]{3,2,1,0:T(8,128)(2,1)} %get-tuple-element.296), channel_id=1, source_target_pairs={{0,8},{8,16},{16,24},{24,32},{32,40},{40,48},{48,56},{56,64},{64,7... | collective-permute-start | bytes 12582920 | tf_op jit(solution)/shard_map/ppermute | solution.py:29
  347.6 98.9 %collective-permute-start.1 = (bf16[8,16,128,128]{3,2,1,0:T(8,128)(2,1)}, bf16[8,16,128,128]{3,2,1,0:T(8,128)(2,1)}, u32[]{:S(2)}, u32[]{:S(2)}) collective-permute-start(bf16[8,16,128,128]{3,2,1,0:T(8,128)(2,1)} %get-tuple-element.295), channel_id=1, source_target_pairs={{8,0},{16,8},{24,16},{32,24},{40,32},{48,40},{56,48},{64,56},{72,6... | collective-permute-start | bytes 12582920 | tf_op jit(solution)/shard_map/ppermute | solution.py:31
  449.6 16.8 %copy-start.2 = (bf16[48,16,128,128]{3,2,1,0:T(8,128)(2,1)}, bf16[48,16,128,128]{3,2,1,0:T(8,128)(2,1)S(1)}, u32[]{:S(2)}) copy-start(bf16[48,16,128,128]{3,2,1,0:T(8,128)(2,1)S(1)} %constant_dynamic-update-slice_fusion) | copy-start | bytes 75497472
  977.7 3.9 copy-start.5
  1196.9 10.2 collective-permute-start.2
  1200.9 15.6 %collective-permute-start.3 = (f32[8,128,128]{2,1,0:T(8,128)S(1)}, f32[8,128,128]{2,1,0:T(8,128)S(1)}, u32[]{:S(2)}, u32[]{:S(2)}) collective-permute-start(f32[8,128,128]{2,1,0:T(8,128)S(1)} %get-tuple-element.297), channel_id=1, source_target_pairs={{0,120},{8,0},{16,8},{24,16},{32,24},{40,32},{48,40},{56,48},{64,5... | collective-permute-start | bytes 1572872 | tf_op jit(solution)/shard_map/ppermute | solution.py:19
  1216.6 1.0 copy-start.3
  1217.6 36.4 %copy-start.1 = (bf16[128,256]{1,0:T(8,128)(2,1)S(1)}, bf16[128,256]{1,0:T(8,128)(2,1)}, u32[]{:S(2)}) copy-start(bf16[128,256]{1,0:T(8,128)(2,1)} %param.17) | copy-start | bytes 196612
Sparse Core Ops, SparseCore 0:
  9.7 328.8 all-gather.1
  1217.8 36.1 reduce-scatter.1
where the time goes:
time: 1270 us; the launch traced here: 1260 us
  waiting for transfers between devices  463 us (36%)
  local copies, waits for them, and re-layouts  452 us (36%)
  matrix products  203 us (16%)
  loops' own time  106 us (8%)
  other arithmetic  15.1 us (1%)
  between operations  14.2 us (1%)
    all_gather x1, waiting for transfers between devices, per_device(): full_rows = lax.all_gather(blocks, 'col', axis=1, tiled=True)  331 us
    gather x32, local copies, waits for them, and re-layouts, one_row(): picked = stacked[block_index]  285 us
    another operation x1, loops' own time, per_device(): square = lax.map(one_row, jnp.arange(rows_dev, dtype=jnp.int32))  105 us
    ppermute x1, waiting for transfers between devices, extended_2(): lax.ppermute(tail, axis, [(i, (i + 1) % count) for i in range(count)])  85.9 us
    transpose x8, local copies, waits for them, and re-layouts, place_batch(): jnp.einsum('qby,qabz->qayz', row_pick, placed_z, precision=highest)  73.6 us
    dot_general x8, matrix products, place_batch(): jnp.einsum('qby,qabz->qayz', row_pick, placed_z, precision=highest)  71.1 us
    dot_general x32, matrix products, one_row(): jnp.einsum('kmn,ksnp->smp', left_blocks, picked, preferred_element_type=j...  69.6 us
    dot_general x8, matrix products, place_batch(): jnp.einsum('qap,qayz->pyz', plane_pick, placed_y, precision=highest)  45 us
  transfers between devices with their start and end apart: 6, of which 5 were waited for; matrix products, arithmetic and copies ran while one was open for 1% of the time, Pallas kernels for 0%

commit v1 on v0

v1 whole, which is shorter than its diff:
```python
import functools

import jax
import jax.numpy as jnp
from jax import lax
from jax.experimental import pallas as pl
from jax.experimental.pallas import tpu as pltpu
from jax.sharding import PartitionSpec as P

MESH = pl.DeviceIdType.MESH
B = 128
K = 16
H = 8
UNIT = 4
POS = 5
ROWS = 16
COLS = 8
SHARES = 64
NBR = 512
BLOCKS = POS * UNIT * K
ANY = pl.BlockSpec(memory_space=pl.ANY)
VMEM = pl.BlockSpec(memory_space=pltpu.VMEM)
SMEM = pl.BlockSpec(memory_space=pltpu.SMEM)


def col_of_place(place):
    return place


def place_of_col(col):
    return col


def device_of(share, core):
    share = lax.rem(share + SHARES, SHARES)
    return 2 * (share // 8) + core, col_of_place(lax.rem(share, 8))


def signal(sem, row, col):
    pl.semaphore_signal(sem, inc=1, device_id=(row, col), device_id_type=MESH)


def gather_kernel(blocks, out, send_sem, recv_sem, fwd_send, fwd_recv):
    row = lax.axis_index("row")
    col = lax.axis_index("col")
    core = lax.rem(row, 2)
    share = (row // 2) * 8 + place_of_col(col)
    partner = (row + 1 - 2 * core, col)

    barrier = pltpu.get_barrier_semaphore()
    first_unit = 2 * share - 2 + 3 * core + 128
    row_a = lax.rem(first_unit // 8, ROWS)
    row_b = lax.rem((first_unit + 2) // 8, ROWS)

    @pl.loop(0, COLS)
    def _(c):
        @pl.when(jnp.logical_or(row_a != row, c != col))
        def _():
            signal(barrier, row_a, c)

        @pl.when(jnp.logical_and(row_b != row_a, jnp.logical_or(row_b != row, c != col)))
        def _():
            signal(barrier, row_b, c)

    signal(barrier, *partner)
    place = lax.rem(share, 8)
    is_own = jnp.where(core == 0, place <= 4, place >= 3).astype(jnp.int32)
    pl.semaphore_wait(barrier, 11 - is_own)

    plan = []
    for u in range(8):
        share_u = 4 * row + u // 2
        if u % 2 == 0:
            goals = [(0, -1, 1, 1), (1, 0, 0, 2), (2, 1, 0, 0)]
        else:
            goals = [(0, 0, 1, 0), (1, 1, 0, 1), (2, -1, 1, 2)]
        for t, step, dest_core, j in goals:
            plan.append((t, u, share_u + step, dest_core, j))
    plan.sort(key=lambda item: (item[0], item[1]))

    def copies(t, u, goal, dest_core, j):
        dest_row, dest_col = device_of(goal, dest_core)
        src = blocks.at[pl.ds(UNIT * u, UNIT)]
        dst = out.at[j + 2 * dest_core, col]
        away = pltpu.make_async_remote_copy(
            src_ref=src,
            dst_ref=dst,
            send_sem=send_sem.at[u, t],
            recv_sem=recv_sem.at[j, col],
            device_id=(dest_row, dest_col),
            device_id_type=MESH,
        )
        here = pltpu.make_async_copy(src, dst, recv_sem.at[j, col])
        is_here = jnp.logical_and(dest_row == row, dest_col == col)
        return away, here, is_here

    for item in plan:
        away, here, is_here = copies(*item)

        @pl.when(is_here)
        def _():
            here.start()

        @pl.when(jnp.logical_not(is_here))
        def _():
            away.start()

    def wait_for(j, c):
        slot = out.at[j + 2 * core, c]
        pltpu.make_async_copy(slot, slot, recv_sem.at[j, c]).wait()

    def forward(f, c):
        return pltpu.make_async_remote_copy(
            src_ref=out.at[1 + core + f, c],
            dst_ref=out.at[3 * core + f, c],
            send_sem=fwd_send.at[f, c],
            recv_sem=fwd_recv.at[f, c],
            device_id=partner,
            device_id_type=MESH,
        )

    for f in range(2):

        @pl.loop(0, COLS)
        def _(c):
            wait_for(f + 1 - core, c)
            forward(f, c).start()

    @pl.loop(0, COLS)
    def _(c):
        wait_for(2 * core, c)

    for f in range(2):

        @pl.loop(0, COLS)
        def _(c):
            forward(f, c).wait()

    for item in plan:
        away, here, is_here = copies(*item)

        @pl.when(jnp.logical_not(is_here))
        def _():
            away.wait_send()


def gather(blocks):
    return pl.pallas_call(
        gather_kernel,
        out_shape=jax.ShapeDtypeStruct((POS, COLS, UNIT, 2, B, B), jnp.bfloat16),
        in_specs=[ANY],
        out_specs=ANY,
        scratch_shapes=[
            pltpu.SemaphoreType.DMA((8, 3)),
            pltpu.SemaphoreType.DMA((3, COLS)),
            pltpu.SemaphoreType.DMA((2, COLS)),
            pltpu.SemaphoreType.DMA((2, COLS)),
        ],
        compiler_params=pltpu.CompilerParams(collective_id=0, has_side_effects=True),
        name="gather_rows",
    )(blocks)


def square_kernel(
    index, corners, blocks, planes, cells, density, mid, low, high, held, halves, tiles, slab, sem
):
    load = pltpu.make_async_copy(blocks, held.at[pl.ds(0, BLOCKS)], sem)
    load.start()
    held[BLOCKS] = jnp.zeros((B, B), jnp.bfloat16)

    @pl.loop(0, 128)
    def _(y):
        slab[y] = jnp.zeros((32, 128), jnp.float32)

    load.wait()

    @pl.loop(0, UNIT)
    def _(i):
        @pl.loop(0, K // 2)
        def _(pair):
            total = jnp.zeros((B, 2 * B), jnp.float32)
            for kk in range(K // 2):
                first = (2 * COLS + kk) * 2 * UNIT + 2 * i
                left = jnp.concatenate([held[first], held[first + 1]], axis=1)
                at = (i * K + 2 * pair) * K + 2 * kk
                right = jnp.concatenate(
                    [
                        jnp.concatenate([held[index[at]], held[index[at + K]]], axis=1),
                        jnp.concatenate([held[index[at + 1]], held[index[at + K + 1]]], axis=1),
                    ],
                    axis=0,
                )
                total += jnp.dot(left, right, preferred_element_type=jnp.float32)
            rounded = total.astype(jnp.bfloat16)
            for e in range(2):
                block = rounded[:, e * B : (e + 1) * B]
                density[pair, i, e] = block
                tile = 2 * pair + e
                placed = pltpu.roll(planes[...], corners[i * K + tile], 0).astype(jnp.bfloat16)
                half = jnp.dot(placed, block, preferred_element_type=jnp.float32)
                halves[pl.ds(pl.multiple_of(tile * 32, 32), 32), :] = half.astype(jnp.bfloat16)

        for b in range(0, 16, 2):
            tiles[:, b * 128 : (b + 2) * 128] = jnp.dot(
                halves[...], cells[:, b * 128 : (b + 2) * 128], preferred_element_type=jnp.float32
            )

        @pl.loop(0, K)
        def _(tile):
            y = corners[UNIT * K + i * K + tile]
            z = corners[2 * UNIT * K + i * K + tile]
            rows = pl.ds(pl.multiple_of(tile * 32, 32), 32)
            for b in range(16):
                slab[y + b] += pltpu.roll(tiles[rows, b * 128 : (b + 1) * 128], z, 1)

    @pl.loop(0, 64)
    def _(y):
        for e in range(2):
            mid[2 * y + e] = slab[2 * y + e, 8:24, :].astype(jnp.bfloat16)
        low[y] = jnp.concatenate([slab[2 * y, 0:8, :], slab[2 * y + 1, 0:8, :]], axis=0).astype(jnp.bfloat16)
        high[y] = jnp.concatenate([slab[2 * y, 24:32, :], slab[2 * y + 1, 24:32, :]], axis=0).astype(
            jnp.bfloat16
        )


def square_rows(index, corners, blocks, planes, cells):
    return pl.pallas_call(
        square_kernel,
        out_shape=[
            jax.ShapeDtypeStruct((COLS, UNIT, 2, B, B), jnp.bfloat16),
            jax.ShapeDtypeStruct((128, 16, 128), jnp.bfloat16),
            jax.ShapeDtypeStruct((64, 16, 128), jnp.bfloat16),
            jax.ShapeDtypeStruct((64, 16, 128), jnp.bfloat16),
        ],
        in_specs=[SMEM, SMEM, ANY, VMEM, VMEM],
        out_specs=[VMEM] * 4,
        scratch_shapes=[
            pltpu.VMEM((BLOCKS + 1, B, B), jnp.bfloat16),
            pltpu.VMEM((K * 32, B), jnp.bfloat16),
            pltpu.VMEM((K * 32, 16 * 128), jnp.float32),
            pltpu.VMEM((128, 32, 128), jnp.float32),
            pltpu.SemaphoreType.DMA,
        ],
        compiler_params=pltpu.CompilerParams(vmem_limit_bytes=48 << 20),
        name="square_rows",
    )(index, corners, blocks, planes, cells)


def return_kernel(density, mid, low, high, square, own, below, above, send_sem, recv_sem):
    row = lax.axis_index("row")
    col = lax.axis_index("col")
    core = lax.rem(row, 2)
    unit = 2 * ((row // 2) * 8 + place_of_col(col)) + core
    owner = unit // 8
    u = lax.rem(unit, 8)
    up = lax.rem(owner + 1, ROWS)
    down = lax.rem(owner + ROWS - 1, ROWS)

    barrier = pltpu.get_barrier_semaphore()

    @pl.loop(0, 24)
    def _(v):
        n = 8 * (row - 1) + v + 128
        from_row, from_col = device_of(n // 2, lax.rem(n, 2))

        @pl.when(jnp.logical_or(from_row != row, from_col != col))
        def _():
            signal(barrier, from_row, from_col)

    pl.semaphore_wait(barrier, 23)

    def pieces(c):
        kinds = [
            (density.at[c], square.at[pl.ds(UNIT * u, UNIT)], owner),
            (mid.at[pl.ds(16 * c, 16)], own.at[u], owner),
            (low.at[pl.ds(8 * c, 8)], above.at[u], down),
            (high.at[pl.ds(8 * c, 8)], below.at[u], up),
        ]
        for kind, (src, dst, to_row) in enumerate(kinds):
            away = pltpu.make_async_remote_copy(
                src_ref=src,
                dst_ref=dst,
                send_sem=send_sem.at[kind, c],
                recv_sem=recv_sem.at[kind, u],
                device_id=(to_row, c),
                device_id_type=MESH,
            )
            here = pltpu.make_async_copy(src, dst, recv_sem.at[kind, u])
            yield away, here, jnp.logical_and(to_row == row, c == col)

    @pl.loop(0, COLS)
    def _(step):
        for away, here, is_here in pieces(lax.rem(col + step, COLS)):

            @pl.when(is_here)
            def _():
                here.start()

            @pl.when(jnp.logical_not(is_here))
            def _():
                away.start()

    @pl.loop(0, 8)
    def _(v):
        for kind, ref in enumerate((square.at[pl.ds(UNIT * v, UNIT)], own.at[v], above.at[v], below.at[v])):
            pltpu.make_async_copy(ref, ref, recv_sem.at[kind, v]).wait()

    @pl.loop(0, COLS)
    def _(step):
        for away, here, is_here in pieces(lax.rem(col + step, COLS)):

            @pl.when(jnp.logical_not(is_here))
            def _():
                away.wait_send()


def give_back(density, mid, low, high):
    return pl.pallas_call(
        return_kernel,
        out_shape=[
            jax.ShapeDtypeStruct((32, 2, B, B), jnp.bfloat16),
            jax.ShapeDtypeStruct((8, 16, 16, 128), jnp.bfloat16),
            jax.ShapeDtypeStruct((8, 8, 16, 128), jnp.bfloat16),
            jax.ShapeDtypeStruct((8, 8, 16, 128), jnp.bfloat16),
        ],
        in_specs=[ANY] * 4,
        out_specs=[ANY] * 4,
        scratch_shapes=[pltpu.SemaphoreType.DMA((4, COLS)), pltpu.SemaphoreType.DMA((4, 8))],
        compiler_params=pltpu.CompilerParams(collective_id=1, has_side_effects=True),
        name="give_back",
    )(density, mid, low, high)


def tables(pattern, anchors, unit):
    first = UNIT * unit
    around = jnp.concatenate([pattern[NBR - H :], pattern, pattern[: UNIT + H]], axis=0)
    window = lax.dynamic_slice_in_dim(around, first, UNIT + 2 * H, 0)
    columns = window[H : H + UNIT]
    rel = jnp.arange(UNIT + 2 * H, dtype=jnp.int32)
    row_ids = (first - H + rel + NBR) % NBR
    slots = jnp.arange(K, dtype=jnp.int32)
    places = ((rel[:, None] // 4) * 8 + slots[None, :] // 2) * 8 + (rel[:, None] % 4) * 2 + slots[None, :] % 2
    found = jnp.sum(
        jnp.where(window[None, None] == columns[:, :, None, None], places[None, None] + 1, 0), axis=3
    )
    is_row = columns[:, :, None] == row_ids[None, None, :]
    index = jnp.sum(jnp.where(is_row[:, None, :, :], found[:, :, None, :], 0), axis=3)
    index = jnp.where(index == 0, BLOCKS, index - 1)
    corner = lax.dynamic_slice(anchors, (0, first, 0), (3, UNIT, K))
    group = unit // 8
    planes = (corner[0] - 16 * group + 8 + 256) % 256
    corners = jnp.concatenate([planes[None], corner[1:]], axis=0)
    return index.reshape(-1), corners.reshape(-1)


def per_device(blocks, pattern, anchors, basis_x, basis_yz):
    row = lax.axis_index("row")
    col = lax.axis_index("col")
    unit = 2 * ((row // 2) * 8 + place_of_col(col)) + row % 2
    index, corners = tables(pattern, anchors, unit)
    planes = jnp.concatenate([basis_x, jnp.zeros_like(basis_x)], axis=0).astype(jnp.float32)
    cells = jnp.pad(basis_yz.reshape(B, 16, 16), ((0, 0), (0, 0), (0, 112))).reshape(B, 16 * 128)
    gathered = gather(blocks).reshape(BLOCKS, B, B)
    density, mid, low, high = square_rows(index, corners, gathered, planes, cells)
    square, own, below, above = give_back(density, mid, low, high)
    total = jnp.sum(own.astype(jnp.float32), axis=0)
    low_sum = jnp.sum(below.astype(jnp.float32), axis=0).reshape(16, 8, 128)
    high_sum = jnp.sum(above.astype(jnp.float32), axis=0).reshape(16, 8, 128)
    total = total + jnp.concatenate([low_sum, high_sum], axis=1)
    return square.astype(jnp.float32), jnp.transpose(total, (1, 0, 2))


def solution(mesh):
    placed = (P("row", "col", None, None), P(), P(), P(), P())
    return jax.shard_map(
        per_device,
        mesh=mesh,
        in_specs=placed,
        out_specs=(P("row", "col", None, None), P("row", "col", None)),
        check_vma=False,
    )
```

time: 1270 us -> 190 us (0.15)
  waiting for transfers between devices: 463 us -> 0 us
  local copies, waits for them, and re-layouts: 452 us -> 8.18 us
  matrix products: 203 us -> 0 us
  Pallas kernels: 0 us -> 168 us
  loops' own time: 106 us -> 0 us
  between operations: 14.2 us -> 0.8 us
    all_gather x1 -> x0, waiting for transfers between devices: 331 us -> none  [per_device(): full_rows = lax.all_gather(blocks, 'col', axis=1, tiled=True)]
    gather x64 -> x0, local copies, waits for them, and re-layouts: 303 us -> none  [the longest x32 285 us: one_row(): picked = stacked[block_index]]
    dot_general x57 -> x0, matrix products: 203 us -> none  [the longest x8 71.1 us: place_batch(): jnp.einsum('qby,qabz->qayz', row_pick, placed_z, precision=highest)]
    pallas_call x0 -> x3, Pallas kernels: none -> 168 us  [the longest x1 86.1 us: gather(): pl.pallas_call(gather_kernel, out_shape=jax.ShapeDtypeStruct((POS, COLS,...]
    another operation x2 -> x0, loops' own time: 106 us -> none  [the longest x1 105 us: per_device(): square = lax.map(one_row, jnp.arange(rows_dev, dtype=jnp.int32))]
    ppermute x4 -> x0, waiting for transfers between devices: 101 us -> none  [the longest x1 85.9 us: extended_2(): lax.ppermute(tail, axis, [(i, (i + 1) % count) for i in range(count)])]
    transpose x8 -> x0, local copies, waits for them, and re-layouts: 73.6 us -> none  [place_batch(): jnp.einsum('qby,qabz->qayz', row_pick, placed_z, precision=highest)]
    reduce_scatter x1 -> x0, waiting for transfers between devices: 30.7 us -> none  [share_sums(): return lax.psum_scatter(slab, 'col', scatter_dimension=1, tiled=True)]
  transfers between devices with their start and end apart: 6 -> 0, of which waited for: 5 -> 0; matrix products, arithmetic and copies ran while one was open for 1% -> 0% of each run, Pallas kernels for 0% -> 0%
where the time goes in v1:
time: 190 us; the launch traced here: 188 us
  Pallas kernels  168 us (88%)
  other arithmetic  11.1 us (6%)
  local copies, waits for them, and re-layouts  8.18 us (4%)
    pallas_call x1, Pallas kernels, gather(): pl.pallas_call(gather_kernel, out_shape=jax.ShapeDtypeStruct((POS, COLS,...  86.1 us
    pallas_call x1, Pallas kernels, give_back(): pl.pallas_call(return_kernel, out_shape=[jax.ShapeDtypeStruct((32, 2, B,...  50.6 us
    pallas_call x1, Pallas kernels, square_rows(): pl.pallas_call(square_kernel, out_shape=[jax.ShapeDtypeStruct((COLS, UNIT...  31.5 us
    unnamed x10, local copies, waits for them, and re-layouts  5.18 us
    convert_element_type x1, other arithmetic, per_device(): return (square.astype(jnp.float32), jnp.transpose(total, (1, 0, 2)))  4.13 us

profile of v1, /device:TPU:1, one launch (start us, length us, event | category | flops | bytes accessed | tf_op | source)
XLA Modules:
  0.0 188.3 jit_solution(10654708958571173144)
XLA Ops:
  0.7 0.1 add_add_fusion
  0.8 0.8 add_select_fusion.1
  1.6 0.8 slice.15
  2.3 0.7 slice.16
  3.0 0.8 fusion.3
  3.8 0.1 slice.20
  3.9 0.1 copy.17
  4.0 0.1 broadcast_compare_fusion
  4.1 0.2 select_reduce_fusion.1
  4.3 1.2 select_reduce_fusion
  5.5 0.1 select_n.106.index
  5.5 0.8 constant_dynamic-slice_fusion
  6.3 0.1 copy.19
  6.4 0.1 reshape.217.corners
  6.5 0.7 pad_convert_fusion.planes
  7.2 0.9 copy.20
  8.2 0.1 pad.5
  8.3 0.2 copy.23.cells
  8.5 86.1 %gather_rows.1 = bf16[5,8,4,2,128,128]{5,4,3,2,1,0:T(8,128)(2,1)} custom-call(bf16[32,2,128,128]{3,2,1,0:T(8,128)(2,1)} %blocks.1), custom_call_target="tpu_custom_call" | custom-call | tf_op jit(solution)/shard_map/gather_rows/pallas_call | solution.py:148
  94.6 31.5 %square_rows.1 = (bf16[8,4,2,128,128]{4,3,2,1,0:T(8,128)(2,1)S(1)}, bf16[128,16,128]{2,1,0:T(8,128)(2,1)S(1)}, bf16[64,16,128]{2,1,0:T(8,128)(2,1)S(1)}, bf16[64,16,128]{2,1,0:T(8,128)(2,1)S(1)}) custom-call(s32[1024]{0:T(1024)S(1)} %select_n.106.index, s32[192]{0:T(256)S(1)} %reshape.217.corners, bf16[320,128,128]{2,1,0:T(8,128)(2,1)} %bitcast.7, ...), custom_call_target="tpu_custom_call" | custom-call | tf_op jit(solution)/shard_map/square_rows/pallas_call | solution.py:227
  126.1 0.0 copy-start
  126.1 1.3 copy-done
  127.5 0.0 copy-start.1
  127.5 0.8 copy-done.1
  128.3 0.0 copy-start.2
  128.3 0.7 copy-done.2
  129.0 0.0 copy-start.3
  129.0 0.7 copy-done.3
  129.7 50.6 %give_back.1 = (bf16[32,2,128,128]{3,2,1,0:T(8,128)(2,1)}, bf16[8,16,16,128]{3,2,1,0:T(8,128)(2,1)}, bf16[8,8,16,128]{3,2,1,0:T(8,128)(2,1)}, bf16[8,8,16,128]{3,2,1,0:T(8,128)(2,1)}) custom-call(bf16[8,4,2,128,128]{4,3,2,1,0:T(8,128)(2,1)} %copy-done, bf16[128,16,128]{2,1,0:T(8,128)(2,1)} %copy-done.1, bf16[64,16,128]{2,1,0:T(8,128)(2,1)} %copy-done.2, ...), custom_call_target="tpu_custom_call" | custom-call | tf_op jit(solution)/shard_map/give_back/pallas_call | solution.py:318
  180.3 1.0 convert_reduce_fusion.2
  181.3 1.0 convert_reduce_fusion.1
  182.3 1.1 convert_reduce_fusion
  183.5 0.7 copy.22
  184.2 4.1 %convert_element_type.18 = f32[32,2,128,128]{3,2,1,0:T(8,128)} convert(bf16[32,2,128,128]{3,2,1,0:T(8,128)(2,1)} %get-tuple-element.14) | non-fusion elementwise | flops 1048576 | bytes 6291456 | tf_op jit(solution)/shard_map/convert_element_type | solution.py:370
  (6 shorter events, 0.1 us)
Async XLA Ops:
  126.1 1.3 copy-start
  127.5 0.8 copy-start.1
  128.3 0.7 copy-start.2
  129.0 0.7 copy-start.3

commit v2 on v0

v2 whole, which is shorter than its diff:
```python
import jax
import jax.numpy as jnp
import numpy as np
from jax import lax
from jax.experimental import pallas as pl
from jax.experimental.pallas import tpu as pltpu
from jax.sharding import PartitionSpec as P

MESH = pl.DeviceIdType.MESH
B = 128
K = 16
H = 8
UNIT = 4
ROWS = 16
COLS = 8
SHARES = 64
NBR = 512
HELD = UNIT * K
ORDER = ((2, 1, 3, 4, 0), (2, 3, 1, 0, 4))
LEFT = 5 * UNIT * UNIT * K
ANY = pl.BlockSpec(memory_space=pl.ANY)
VMEM = pl.BlockSpec(memory_space=pltpu.VMEM)
SMEM = pl.BlockSpec(memory_space=pltpu.SMEM)


def col_of_place(place):
    return place


def place_of_col(col):
    return col


def device_of(share, core):
    share = lax.rem(share + SHARES, SHARES)
    return 2 * (share // 8) + core, col_of_place(lax.rem(share, 8))


def signal(sem, row, col):
    pl.semaphore_signal(sem, inc=1, device_id=(row, col), device_id_type=MESH)


def kernel(
    index, corners, blocks, planes, cells,
    square, grid,
    held0, held1, held2, held3, held4, sums, density, halves, tiles, mid, low, high, own, below, above, total,
    send_sem, recv_sem, fwd_send, fwd_recv, back_send, back_recv,
):
    row = lax.axis_index("row")
    col = lax.axis_index("col")
    core = lax.rem(row, 2)
    share = (row // 2) * 8 + place_of_col(col)
    partner = (row + 1 - 2 * core, col)
    unit = 2 * share + core
    owner = unit // 8
    u_back = lax.rem(unit, 8)
    up = lax.rem(owner + 1, ROWS)
    down = lax.rem(owner + ROWS - 1, ROWS)
    held = (held0, held1, held2, held3, held4)

    for ref in held:
        ref[HELD] = jnp.zeros((B, B), jnp.bfloat16)
    tiles[1024] = jnp.zeros((32, B), jnp.float32)

    barrier = pltpu.get_barrier_semaphore()
    first_unit = 2 * share - 2 + 3 * core + 128
    row_a = lax.rem(first_unit // 8, ROWS)
    row_b = lax.rem((first_unit + 2) // 8, ROWS)

    @pl.loop(0, COLS)
    def _(c):
        @pl.when(jnp.logical_or(row_a != row, c != col))
        def _():
            signal(barrier, row_a, c)

        @pl.when(jnp.logical_and(row_b != row_a, jnp.logical_or(row_b != row, c != col)))
        def _():
            signal(barrier, row_b, c)

    @pl.loop(0, 24)
    def _(v):
        n = 8 * (row - 1) + v + 128
        from_row, from_col = device_of(n // 2, lax.rem(n, 2))

        @pl.when(jnp.logical_or(from_row != row, from_col != col))
        def _():
            signal(barrier, from_row, from_col)

    signal(barrier, *partner)
    place = lax.rem(share, 8)
    is_own = jnp.where(core == 0, place <= 4, place >= 3).astype(jnp.int32)
    pl.semaphore_wait(barrier, 34 - is_own)

    plan = ((0, 1, 0, 1), (0, 0, 0, 0), (1, 0, -1, 1), (1, 1, 1, 0), (2, 0, 1, 0), (2, 1, -1, 1))

    def sends(v, kind, parity, step, goal_core):
        u = 2 * v + parity
        goal_row, goal_col = device_of(4 * row + v + step, goal_core)
        src = blocks.at[pl.ds(2 * UNIT * u, 2 * UNIT)]
        dst = held[4 if kind == 2 else kind].at[pl.ds(2 * UNIT * col, 2 * UNIT)]
        away = pltpu.make_async_remote_copy(
            src_ref=src,
            dst_ref=dst,
            send_sem=send_sem.at[u, kind],
            recv_sem=recv_sem.at[kind, col],
            device_id=(goal_row, goal_col),
            device_id_type=MESH,
        )
        is_here = jnp.logical_and(goal_row == row, goal_col == col)
        return src, dst, recv_sem.at[kind, col], away, is_here

    for half in range(3):

        @pl.loop(0, 4)
        def _(w):
            v = lax.rem(w + col, 4)
            for item in plan[2 * half : 2 * half + 2]:
                src, dst, sem, away, is_here = sends(v, *item)

                @pl.when(is_here)
                def _():
                    pltpu.make_async_copy(src, dst, sem).start()

                @pl.when(jnp.logical_not(is_here))
                def _():
                    away.start()

    def part(ref, c):
        return ref.at[pl.ds(2 * UNIT * c, 2 * UNIT)]

    def forward(f, c):
        return pltpu.make_async_remote_copy(
            src_ref=part(held[f], c),
            dst_ref=part(held[2 + f], c),
            send_sem=fwd_send.at[f, c],
            recv_sem=fwd_recv.at[f, c],
            device_id=partner,
            device_id_type=MESH,
        )

    def wait_for(kind, c):
        slot = part(held[4 if kind == 2 else kind], c)
        pltpu.make_async_copy(slot, slot, recv_sem.at[kind, c]).wait()

    for f in range(2):

        @pl.loop(0, COLS)
        def _(c):
            wait_for(f, c)
            forward(f, c).start()

    def product(rank, i, pair):
        out = jnp.zeros((B, 2 * B), jnp.float32)
        for kk in range(0, UNIT, 2):
            lefts = [held0[index[LEFT + (rank * UNIT + kk + e) * UNIT + i]] for e in range(2)]
            rights = []
            for e in range(2):
                at = ((rank * UNIT + kk + e) * UNIT + i) * K + 2 * pair
                rights.append(jnp.concatenate([held[rank][index[at]], held[rank][index[at + 1]]], axis=1))
            out += jnp.dot(
                jnp.concatenate(lefts, axis=1), jnp.concatenate(rights, axis=0), preferred_element_type=jnp.float32
            )
        return out

    for rank in range(4):
        if rank >= 2:

            @pl.loop(0, COLS)
            def _(c):
                forward(rank - 2, c).wait()

        @pl.loop(0, UNIT * K // 2)
        def _(at):
            value = product(rank, at // (K // 2), lax.rem(at, K // 2))
            sums[at] = value if rank == 0 else sums[at] + value

    @pl.loop(0, COLS)
    def _(c):
        wait_for(2, c)

    def goes_back(kind, c):
        src, dst, to_row = (
            (density.at[pl.ds(2 * UNIT * c, 2 * UNIT)], square.at[pl.ds(2 * UNIT * u_back, 2 * UNIT)], owner),
            (mid.at[pl.ds(16 * c, 16)], own.at[u_back], owner),
            (low.at[pl.ds(8 * c, 8)], above.at[u_back], down),
            (high.at[pl.ds(8 * c, 8)], below.at[u_back], up),
        )[kind]
        away = pltpu.make_async_remote_copy(
            src_ref=src,
            dst_ref=dst,
            send_sem=back_send.at[kind, c],
            recv_sem=back_recv.at[kind, u_back],
            device_id=(to_row, c),
            device_id_type=MESH,
        )
        return src, dst, back_recv.at[kind, u_back], away, jnp.logical_and(to_row == row, c == col)

    def start_back(kind, c):
        src, dst, sem, away, is_here = goes_back(kind, c)

        @pl.when(is_here)
        def _():
            pltpu.make_async_copy(src, dst, sem).start()

        @pl.when(jnp.logical_not(is_here))
        def _():
            away.start()

    @pl.loop(0, COLS)
    def _(w):
        pair = lax.rem(w + col, COLS)

        @pl.loop(0, UNIT)
        def _(i):
            value = (sums[i * (K // 2) + pair] + product(4, i, pair)).astype(jnp.bfloat16)
            for e in range(2):
                density[2 * UNIT * pair + 2 * i + e] = value[:, e * B : (e + 1) * B]

        start_back(0, pair)

    @pl.loop(0, UNIT)
    def _(i):
        @pl.loop(0, K // 2)
        def _(pair):
            for e in range(2):
                tile = 2 * pair + e
                placed = pltpu.roll(planes[...], corners[i * K + tile], 0).astype(jnp.bfloat16)
                half = jnp.dot(placed, density[2 * UNIT * pair + 2 * i + e], preferred_element_type=jnp.float32)
                halves[pl.ds(pl.multiple_of(tile * 32, 32), 32), :] = half.astype(jnp.bfloat16)

        @pl.loop(0, K // 4)
        def _(four):
            rows = pl.ds(pl.multiple_of(four * 128, 128), 128)
            shifts = [corners[2 * UNIT * K + i * K + 4 * four + e] for e in range(4)]
            for b in range(0, 16, 2):
                values = jnp.dot(
                    halves[rows, :], cells[:, b * 128 : (b + 2) * 128], preferred_element_type=jnp.float32
                )
                for e in range(4):
                    for f in range(2):
                        piece = values[e * 32 : (e + 1) * 32, f * 128 : (f + 1) * 128]
                        tiles[(i * K + 4 * four + e) * 16 + b + f] = pltpu.roll(piece, shifts[e], 1)

    def plane_sum(y):
        value = jnp.zeros((32, B), jnp.float32)
        for tile in range(UNIT * K):
            off = y - corners[UNIT * K + tile]
            inside = jnp.logical_and(off >= 0, off < 16)
            value += tiles[jnp.where(inside, tile * 16 + off, 1024)]
        return value

    @pl.loop(0, COLS)
    def _(w):
        c = lax.rem(w + col, COLS)

        @pl.loop(0, 8)
        def _(yy):
            at = 8 * c + yy
            both = [plane_sum(2 * at + e) for e in range(2)]
            for e in range(2):
                mid[2 * at + e] = both[e][8:24].astype(jnp.bfloat16)
            low[at] = jnp.concatenate([both[0][0:8], both[1][0:8]], axis=0).astype(jnp.bfloat16)
            high[at] = jnp.concatenate([both[0][24:32], both[1][24:32]], axis=0).astype(jnp.bfloat16)

        for kind in (1, 2, 3):
            start_back(kind, c)

    @pl.loop(0, 8)
    def _(v):
        refs = (square.at[pl.ds(2 * UNIT * v, 2 * UNIT)], own.at[v], above.at[v], below.at[v])
        for kind, ref in enumerate(refs):
            pltpu.make_async_copy(ref, ref, back_recv.at[kind, v]).wait()

    def added(ref, at):
        value = ref[0, at].astype(jnp.float32)
        for v in range(1, 8):
            value += ref[v, at].astype(jnp.float32)
        return value

    @pl.loop(0, 8)
    def _(yy):
        under, over = added(below, yy), added(above, yy)
        for e in range(2):
            rims = jnp.concatenate([under[8 * e : 8 * e + 8], over[8 * e : 8 * e + 8]], axis=0)
            at = pl.multiple_of((2 * yy + e) * 16, 16)
            total[pl.ds(at, 16), :] = added(own, 2 * yy + e) + rims

    for x in range(16):
        grid[x] = total[pl.ds(x, 16, stride=16), :]

    @pl.loop(0, 4)
    def _(v):
        for item in plan:
            away, is_here = sends(v, *item)[3:]

            @pl.when(jnp.logical_not(is_here))
            def _():
                away.wait_send()

    @pl.loop(0, COLS)
    def _(c):
        for kind in range(4):
            away, is_here = goes_back(kind, c)[3:]

            @pl.when(jnp.logical_not(is_here))
            def _():
                away.wait_send()


def fused(index, corners, blocks, planes, cells):
    return pl.pallas_call(
        kernel,
        out_shape=[
            jax.ShapeDtypeStruct((64, B, B), jnp.bfloat16),
            jax.ShapeDtypeStruct((16, 16, 128), jnp.float32),
        ],
        in_specs=[SMEM, SMEM, ANY, VMEM, VMEM],
        out_specs=[ANY, VMEM],
        scratch_shapes=[pltpu.VMEM((HELD + 1, B, B), jnp.bfloat16)] * 5
        + [
            pltpu.VMEM((UNIT * K // 2, B, 2 * B), jnp.float32),
            pltpu.VMEM((HELD, B, B), jnp.bfloat16),
            pltpu.VMEM((K * 32, B), jnp.bfloat16),
            pltpu.VMEM((1025, 32, 128), jnp.float32),
            pltpu.VMEM((128, 16, 128), jnp.bfloat16),
            pltpu.VMEM((64, 16, 128), jnp.bfloat16),
            pltpu.VMEM((64, 16, 128), jnp.bfloat16),
            pltpu.VMEM((8, 16, 16, 128), jnp.bfloat16),
            pltpu.VMEM((8, 8, 16, 128), jnp.bfloat16),
            pltpu.VMEM((8, 8, 16, 128), jnp.bfloat16),
            pltpu.VMEM((256, 128), jnp.float32),
            pltpu.SemaphoreType.DMA((8, 3)),
            pltpu.SemaphoreType.DMA((3, COLS)),
            pltpu.SemaphoreType.DMA((2, COLS)),
            pltpu.SemaphoreType.DMA((2, COLS)),
            pltpu.SemaphoreType.DMA((4, COLS)),
            pltpu.SemaphoreType.DMA((4, 8)),
        ],
        compiler_params=pltpu.CompilerParams(collective_id=0, has_side_effects=True, vmem_limit_bytes=52 << 20),
        name="square_and_tiles",
    )(index, corners, blocks, planes, cells)


def tables(pattern, anchors, unit):
    first = UNIT * unit
    around = jnp.concatenate([pattern[NBR - H :], pattern, pattern[: UNIT + H]], axis=0)
    window = lax.dynamic_slice_in_dim(around, first, UNIT + 2 * H, 0)
    columns = window[H : H + UNIT]
    picks = [np.concatenate([np.arange(UNIT) + UNIT * pos for pos in order]) for order in ORDER]
    on_first = unit % 2 == 0
    far = jnp.where(on_first, window[picks[0]], window[picks[1]])
    far_ids = (first - H + jnp.where(on_first, picks[0], picks[1]) + NBR) % NBR
    slots = jnp.arange(K, dtype=jnp.int32)
    inner = jnp.arange(5 * UNIT, dtype=jnp.int32) % UNIT
    place = (slots // 2) * 8 + slots % 2 + 1
    right = jnp.sum(
        jnp.where(
            far[:, None, None, :] == columns[None, :, :, None], (place + 2 * inner[:, None])[:, None, None, :], 0
        ),
        axis=3,
    )
    rows = jnp.arange(UNIT, dtype=jnp.int32)
    left = jnp.sum(
        jnp.where(columns[None] == far_ids[:, None, None], (place + 2 * rows[:, None])[None], 0), axis=2
    )
    index = jnp.concatenate([right.reshape(-1), left.reshape(-1)])
    index = jnp.where(index == 0, HELD, index - 1)
    corner = lax.dynamic_slice(anchors, (0, first, 0), (3, UNIT, K))
    planes = (corner[0] - 16 * (unit // 8) + 8 + 256) % 256
    corners = jnp.concatenate([planes[None], corner[1:]], axis=0)
    return index, corners.reshape(-1)


def per_device(blocks, pattern, anchors, basis_x, basis_yz):
    row = lax.axis_index("row")
    col = lax.axis_index("col")
    unit = 2 * ((row // 2) * 8 + place_of_col(col)) + row % 2
    index, corners = tables(pattern, anchors, unit)
    planes = jnp.concatenate([basis_x, jnp.zeros_like(basis_x)], axis=0).astype(jnp.float32)
    cells = jnp.pad(basis_yz.reshape(B, 16, 16), ((0, 0), (0, 0), (0, 112))).reshape(B, 16 * 128)
    square, grid = fused(index, corners, blocks.reshape(64, B, B), planes, cells)
    return square.reshape(32, 2, B, B).astype(jnp.float32), grid


def solution(mesh):
    placed = (P("row", "col", None, None), P(), P(), P(), P())
    return jax.shard_map(
        per_device,
        mesh=mesh,
        in_specs=placed,
        out_specs=(P("row", "col", None, None), P("row", "col", None)),
        check_vma=False,
    )
```

time: 1270 us -> 175 us (0.14)
  waiting for transfers between devices: 463 us -> 0 us
  local copies, waits for them, and re-layouts: 452 us -> 6.06 us
  matrix products: 203 us -> 0 us
  Pallas kernels: 0 us -> 158 us
  loops' own time: 106 us -> 0 us
  between operations: 14.2 us -> 0.8 us
    all_gather x1 -> x0, waiting for transfers between devices: 331 us -> none  [per_device(): full_rows = lax.all_gather(blocks, 'col', axis=1, tiled=True)]
    gather x64 -> x2, local copies, waits for them, and re-layouts: 303 us -> 1.13 us  [tables(): far = jnp.where(on_first, window[picks[0]], window[picks[1]])]
    dot_general x57 -> x0, matrix products: 203 us -> none  [the longest x8 71.1 us: place_batch(): jnp.einsum('qby,qabz->qayz', row_pick, placed_z, precision=highest)]
    pallas_call x0 -> x1, Pallas kernels: none -> 158 us  [fused(): pl.pallas_call(kernel, out_shape=[jax.ShapeDtypeStruct((64, B, B), jnp.bf...]
    another operation x2 -> x0, loops' own time: 106 us -> none  [the longest x1 105 us: per_device(): square = lax.map(one_row, jnp.arange(rows_dev, dtype=jnp.int32))]
    ppermute x4 -> x0, waiting for transfers between devices: 101 us -> none  [the longest x1 85.9 us: extended_2(): lax.ppermute(tail, axis, [(i, (i + 1) % count) for i in range(count)])]
    transpose x8 -> x0, local copies, waits for them, and re-layouts: 73.6 us -> none  [place_batch(): jnp.einsum('qby,qabz->qayz', row_pick, placed_z, precision=highest)]
    reduce_scatter x1 -> x0, waiting for transfers between devices: 30.7 us -> none  [share_sums(): return lax.psum_scatter(slab, 'col', scatter_dimension=1, tiled=True)]
  transfers between devices with their start and end apart: 6 -> 0, of which waited for: 5 -> 0; matrix products, arithmetic and copies ran while one was open for 1% -> 0% of each run, Pallas kernels for 0% -> 0%
where the time goes in v2:
time: 175 us; the launch traced here: 174 us
  Pallas kernels  158 us (90%)
  other arithmetic  8.87 us (5%)
  local copies, waits for them, and re-layouts  6.06 us (3%)
    pallas_call x1, Pallas kernels, fused(): pl.pallas_call(kernel, out_shape=[jax.ShapeDtypeStruct((64, B, B), jnp.bf...  158 us
    convert_element_type x1, other arithmetic, per_device(): return (square.reshape(32, 2, B, B).astype(jnp.float32), grid)  4.13 us

profile of v2, /device:TPU:1, one launch (start us, length us, event | category | flops | bytes accessed | tf_op | source)
XLA Modules:
  0.0 173.8 jit_solution(12589019225754500525)
XLA Ops:
  0.7 0.7 and_select_fusion
  1.4 0.1 broadcast_add_fusion.1
  1.5 0.7 pad_clamp_fusion.1
  2.1 0.7 pad_clamp_fusion
  2.8 0.1 broadcast_add_fusion
  2.9 0.8 add_select_fusion
  3.6 0.8 slice.15
  4.4 0.7 slice.16
  5.1 0.8 fusion.2
  5.9 0.1 copy.32
  6.0 0.1 select_reduce_fusion.1
  6.1 0.6 gather_fusion.1
  6.7 0.6 gather_fusion
  7.2 0.1 copy.25
  7.3 0.1 copy.27
  7.4 0.1 reshape.123
  7.5 0.2 select_reduce_fusion
  7.7 0.1 copy.26
  7.8 0.1 reshape.122
  8.0 0.8 constant_dynamic-slice_fusion
  8.8 0.1 copy.28
  8.9 0.1 reshape.124.corners
  8.9 0.7 pad_convert_fusion.planes
  9.6 0.9 copy.29
  10.6 0.1 pad.5
  10.7 0.2 copy.31.cells
  10.9 158.0 %square_and_tiles.1 = (bf16[64,128,128]{2,1,0:T(8,128)(2,1)}, f32[16,16,128]{2,1,0:T(8,128)S(1)}) custom-call(s32[1360]{0:T(1024)S(1)} %add_select_fusion.1.index, s32[192]{0:T(256)S(1)} %reshape.124.corners, bf16[64,128,128]{2,1,0:T(8,128)(2,1)} %bitcast.6, f32[32,128]{1,0:T(8,128)S(1)} %pad_convert_fusion.planes, bf16[128,2048]{1,0:T(8,128)(2,1)S(1)} %copy.31.cells), custom_call_target="tpu_custom_call" | custom-call | tf_op jit(solution)/shard_map/square_and_tiles/pallas_call | solution.py:311
  169.0 4.1 %convert.1 = f32[32,2,128,128]{3,2,1,0:T(8,128)} convert(bf16[32,2,128,128]{3,2,1,0:T(8,128)(2,1)} %bitcast.5) | non-fusion elementwise | flops 1048576 | bytes 6291456 | tf_op jit(solution)/shard_map/convert_element_type | solution.py:382
  173.1 0.7 copy.36
  (9 shorter events, 0.0 us)

commit v3 on v2

--- a/solution.py
+++ b/solution.py
@@ -1,6 +1,5 @@
 import jax
 import jax.numpy as jnp
-import numpy as np
 from jax import lax
 from jax.experimental import pallas as pl
 from jax.experimental.pallas import tpu as pltpu
@@ -16,8 +15,10 @@
 SHARES = 64
 NBR = 512
 HELD = UNIT * K
-ORDER = ((2, 1, 3, 4, 0), (2, 3, 1, 0, 4))
-LEFT = 5 * UNIT * UNIT * K
+CORNERS = 5 * UNIT * UNIT
+TABLE = 96
+PAD = 8
+SPAN = 32
 ANY = pl.BlockSpec(memory_space=pl.ANY)
 VMEM = pl.BlockSpec(memory_space=pltpu.VMEM)
 SMEM = pl.BlockSpec(memory_space=pltpu.SMEM)
@@ -41,10 +42,11 @@
 
 
 def kernel(
-    index, corners, blocks, planes, cells,
+    pattern, anchors, blocks, basis_x, basis_yz,
     square, grid,
     held0, held1, held2, held3, held4, sums, density, halves, tiles, mid, low, high, own, below, above, total,
-    send_sem, recv_sem, fwd_send, fwd_recv, back_send, back_recv,
+    rows_held, corners_held, planes, cells, drawn, index,
+    send_sem, recv_sem, fwd_send, fwd_recv, back_send, back_recv, table_sem,
 ):
     row = lax.axis_index("row")
     col = lax.axis_index("col")
@@ -57,10 +59,6 @@
     up = lax.rem(owner + 1, ROWS)
     down = lax.rem(owner + ROWS - 1, ROWS)
     held = (held0, held1, held2, held3, held4)
-
-    for ref in held:
-        ref[HELD] = jnp.zeros((B, B), jnp.bfloat16)
-    tiles[1024] = jnp.zeros((32, B), jnp.float32)
 
     barrier = pltpu.get_barrier_semaphore()
     first_unit = 2 * share - 2 + 3 * core + 128
@@ -113,7 +111,7 @@
 
         @pl.loop(0, 4)
         def _(w):
-            v = lax.rem(w + col, 4)
+            v = lax.rem(w + col // 2, 4)
             for item in plan[2 * half : 2 * half + 2]:
                 src, dst, sem, away, is_here = sends(v, *item)
 
@@ -124,6 +122,65 @@
                 @pl.when(jnp.logical_not(is_here))
                 def _():
                     away.start()
+
+    loads = (
+        pltpu.make_async_copy(pattern, rows_held, table_sem.at[0]),
+        pltpu.make_async_copy(anchors, corners_held, table_sem.at[1]),
+    )
+    for load in loads:
+        load.start()
+    for ref in held:
+        ref[HELD] = jnp.zeros((B, B), jnp.bfloat16)
+
+    planes[...] = jnp.concatenate([basis_x[...].astype(jnp.float32), jnp.zeros((16, B), jnp.float32)], axis=0)
+    lane = lax.broadcasted_iota(jnp.int32, (B, B), 1)
+    for b in range(16):
+        half = basis_yz[:, (b // 8) * B : (b // 8 + 1) * B].astype(jnp.float32)
+        turned = pltpu.roll(half, (B - 16 * (b % 8)) % B, 1)
+        cells[:, b * B : (b + 1) * B] = jnp.where(lane < 16, turned, 0.0).astype(jnp.bfloat16)
+
+    @pl.loop(0, UNIT * K)
+    def _(tile):
+        for e in range(PAD):
+            tiles[tile * SPAN + e] = jnp.zeros((32, B), jnp.float32)
+            tiles[tile * SPAN + PAD + 16 + e] = jnp.zeros((32, B), jnp.float32)
+
+    for load in loads:
+        load.wait()
+    columns = rows_held[pl.ds(UNIT * unit, UNIT), :]
+    own_row = lax.broadcasted_iota(jnp.int32, (UNIT, K), 0)
+    own_slot = lax.broadcasted_iota(jnp.int32, (UNIT, K), 1)
+    own_place = (own_slot // 2) * 8 + lax.rem(own_slot, 2) + 2 * own_row
+    far_slot = lax.broadcasted_iota(jnp.int32, (K, K), 0)
+    far_place = (far_slot // 2) * 8 + lax.rem(far_slot, 2)
+    wide = lax.broadcasted_iota(jnp.int32, (UNIT, B), 1)
+    drawn[...] = jnp.zeros((TABLE, B), jnp.int32)
+    for rank in range(5):
+        step = (0, -1, 1, 2, -2)[rank]
+        far_unit = lax.rem(unit + step * (1 - 2 * core) + 128, 128)
+        for cc in range(UNIT):
+            far = jnp.transpose(jnp.broadcast_to(rows_held[pl.ds(UNIT * far_unit + cc, 1), :], (K, K)))
+            rights = []
+            for i in range(UNIT):
+                fits = far == jnp.broadcast_to(columns[i : i + 1], (K, K))
+                found = jnp.sum(jnp.where(fits, far_place + 2 * cc + 1, 0), axis=0, keepdims=True)
+                rights.append(jnp.where(found == 0, HELD, jnp.minimum(found - 1, HELD)))
+            right = jnp.concatenate(rights, axis=0)
+            found = jnp.sum(
+                jnp.where(columns == UNIT * far_unit + cc, own_place + 1, 0), axis=1, keepdims=True
+            )
+            left = jnp.where(found == 0, HELD, jnp.minimum(found - 1, HELD))
+            at = (rank * UNIT + cc) * UNIT
+            drawn[at : at + UNIT, :] = jnp.where(wide < K, jnp.tile(right, (1, B // K)), left)
+    for d in range(3):
+        corner = corners_held[d, pl.ds(UNIT * unit, UNIT), :]
+        if d == 0:
+            corner = lax.rem(corner - 16 * owner + 8 + 256, 256)
+        at = CORNERS + d * UNIT
+        drawn[at : at + UNIT, 0:K] = corner
+    fetch = pltpu.make_async_copy(drawn, index, table_sem.at[2])
+    fetch.start()
+    fetch.wait()
 
     def part(ref, c):
         return ref.at[pl.ds(2 * UNIT * c, 2 * UNIT)]
@@ -152,11 +209,13 @@
     def product(rank, i, pair):
         out = jnp.zeros((B, 2 * B), jnp.float32)
         for kk in range(0, UNIT, 2):
-            lefts = [held0[index[LEFT + (rank * UNIT + kk + e) * UNIT + i]] for e in range(2)]
+            lefts = [held0[index[(rank * UNIT + kk + e) * UNIT + i, K]] for e in range(2)]
             rights = []
             for e in range(2):
-                at = ((rank * UNIT + kk + e) * UNIT + i) * K + 2 * pair
-                rights.append(jnp.concatenate([held[rank][index[at]], held[rank][index[at + 1]]], axis=1))
+                at = (rank * UNIT + kk + e) * UNIT + i
+                rights.append(
+                    jnp.concatenate([held[rank][index[at, 2 * pair + f]] for f in range(2)], axis=1)
+                )
             out += jnp.dot(
                 jnp.concatenate(lefts, axis=1), jnp.concatenate(rights, axis=0), preferred_element_type=jnp.float32
             )
@@ -224,14 +283,14 @@
         def _(pair):
             for e in range(2):
                 tile = 2 * pair + e
-                placed = pltpu.roll(planes[...], corners[i * K + tile], 0).astype(jnp.bfloat16)
+                placed = pltpu.roll(planes[...], index[CORNERS + i, tile], 0).astype(jnp.bfloat16)
                 half = jnp.dot(placed, density[2 * UNIT * pair + 2 * i + e], preferred_element_type=jnp.float32)
                 halves[pl.ds(pl.multiple_of(tile * 32, 32), 32), :] = half.astype(jnp.bfloat16)
 
         @pl.loop(0, K // 4)
         def _(four):
             rows = pl.ds(pl.multiple_of(four * 128, 128), 128)
-            shifts = [corners[2 * UNIT * K + i * K + 4 * four + e] for e in range(4)]
+            shifts = [index[CORNERS + 2 * UNIT + i, 4 * four + e] for e in range(4)]
             for b in range(0, 16, 2):
                 values = jnp.dot(
                     halves[rows, :], cells[:, b * 128 : (b + 2) * 128], preferred_element_type=jnp.float32
@@ -239,28 +298,31 @@
                 for e in range(4):
                     for f in range(2):
                         piece = values[e * 32 : (e + 1) * 32, f * 128 : (f + 1) * 128]
-                        tiles[(i * K + 4 * four + e) * 16 + b + f] = pltpu.roll(piece, shifts[e], 1)
-
-    def plane_sum(y):
-        value = jnp.zeros((32, B), jnp.float32)
-        for tile in range(UNIT * K):
-            off = y - corners[UNIT * K + tile]
-            inside = jnp.logical_and(off >= 0, off < 16)
-            value += tiles[jnp.where(inside, tile * 16 + off, 1024)]
-        return value
+                        tiles[(i * K + 4 * four + e) * SPAN + PAD + b + f] = pltpu.roll(piece, shifts[e], 1)
 
     @pl.loop(0, COLS)
     def _(w):
         c = lax.rem(w + col, COLS)
 
-        @pl.loop(0, 8)
-        def _(yy):
-            at = 8 * c + yy
-            both = [plane_sum(2 * at + e) for e in range(2)]
-            for e in range(2):
-                mid[2 * at + e] = both[e][8:24].astype(jnp.bfloat16)
-            low[at] = jnp.concatenate([both[0][0:8], both[1][0:8]], axis=0).astype(jnp.bfloat16)
-            high[at] = jnp.concatenate([both[0][24:32], both[1][24:32]], axis=0).astype(jnp.bfloat16)
+        @pl.loop(0, 2)
+        def _(h):
+            eight = 2 * c + h
+
+            def add_tile(tile, values):
+                off = 8 * eight - index[CORNERS + UNIT + tile // K, lax.rem(tile, K)]
+                inside = jnp.logical_and(off > -PAD, off < 16)
+                start = tile * SPAN + jnp.where(inside, off + PAD, 0)
+                return tuple(value + tiles[start + y] for y, value in enumerate(values))
+
+            values = lax.fori_loop(
+                0, UNIT * K, add_tile, tuple(jnp.zeros((32, B), jnp.float32) for _ in range(8)), unroll=2
+            )
+            for y in range(8):
+                mid[8 * eight + y] = values[y][8:24].astype(jnp.bfloat16)
+            for y in range(4):
+                first, second = values[2 * y], values[2 * y + 1]
+                low[4 * eight + y] = jnp.concatenate([first[0:8], second[0:8]], axis=0).astype(jnp.bfloat16)
+                high[4 * eight + y] = jnp.concatenate([first[24:32], second[24:32]], axis=0).astype(jnp.bfloat16)
 
         for kind in (1, 2, 3):
             start_back(kind, c)
@@ -307,21 +369,21 @@
                 away.wait_send()
 
 
-def fused(index, corners, blocks, planes, cells):
+def fused(pattern, anchors, blocks, basis_x, basis_yz):
     return pl.pallas_call(
         kernel,
         out_shape=[
             jax.ShapeDtypeStruct((64, B, B), jnp.bfloat16),
             jax.ShapeDtypeStruct((16, 16, 128), jnp.float32),
         ],
-        in_specs=[SMEM, SMEM, ANY, VMEM, VMEM],
+        in_specs=[ANY, ANY, ANY, VMEM, VMEM],
         out_specs=[ANY, VMEM],
         scratch_shapes=[pltpu.VMEM((HELD + 1, B, B), jnp.bfloat16)] * 5
         + [
             pltpu.VMEM((UNIT * K // 2, B, 2 * B), jnp.float32),
             pltpu.VMEM((HELD, B, B), jnp.bfloat16),
             pltpu.VMEM((K * 32, B), jnp.bfloat16),
-            pltpu.VMEM((1025, 32, 128), jnp.float32),
+            pltpu.VMEM((UNIT * K * SPAN, 32, 128), jnp.float32),
             pltpu.VMEM((128, 16, 128), jnp.bfloat16),
             pltpu.VMEM((64, 16, 128), jnp.bfloat16),
             pltpu.VMEM((64, 16, 128), jnp.bfloat16),
@@ -329,56 +391,27 @@
             pltpu.VMEM((8, 8, 16, 128), jnp.bfloat16),
             pltpu.VMEM((8, 8, 16, 128), jnp.bfloat16),
             pltpu.VMEM((256, 128), jnp.float32),
+            pltpu.VMEM((NBR, K), jnp.int32),
+            pltpu.VMEM((3, NBR, K), jnp.int32),
+            pltpu.VMEM((32, B), jnp.float32),
+            pltpu.VMEM((B, 16 * B), jnp.bfloat16),
+            pltpu.VMEM((TABLE, B), jnp.int32),
+            pltpu.SMEM((TABLE, B), jnp.int32),
             pltpu.SemaphoreType.DMA((8, 3)),
             pltpu.SemaphoreType.DMA((3, COLS)),
             pltpu.SemaphoreType.DMA((2, COLS)),
             pltpu.SemaphoreType.DMA((2, COLS)),
             pltpu.SemaphoreType.DMA((4, COLS)),
             pltpu.SemaphoreType.DMA((4, 8)),
+            pltpu.SemaphoreType.DMA((3,)),
         ],
-        compiler_params=pltpu.CompilerParams(collective_id=0, has_side_effects=True, vmem_limit_bytes=52 << 20),
+        compiler_params=pltpu.CompilerParams(collective_id=0, has_side_effects=True, vmem_limit_bytes=60 << 20),
         name="square_and_tiles",
-    )(index, corners, blocks, planes, cells)
-
-
-def tables(pattern, anchors, unit):
-    first = UNIT * unit
-    around = jnp.concatenate([pattern[NBR - H :], pattern, pattern[: UNIT + H]], axis=0)
-    window = lax.dynamic_slice_in_dim(around, first, UNIT + 2 * H, 0)
-    columns = window[H : H + UNIT]
-    picks = [np.concatenate([np.arange(UNIT) + UNIT * pos for pos in order]) for order in ORDER]
-    on_first = unit % 2 == 0
-    far = jnp.where(on_first, window[picks[0]], window[picks[1]])
-    far_ids = (first - H + jnp.where(on_first, picks[0], picks[1]) + NBR) % NBR
-    slots = jnp.arange(K, dtype=jnp.int32)
-    inner = jnp.arange(5 * UNIT, dtype=jnp.int32) % UNIT
-    place = (slots // 2) * 8 + slots % 2 + 1
-    right = jnp.sum(
-        jnp.where(
-            far[:, None, None, :] == columns[None, :, :, None], (place + 2 * inner[:, None])[:, None, None, :], 0
-        ),
-        axis=3,
-    )
-    rows = jnp.arange(UNIT, dtype=jnp.int32)
-    left = jnp.sum(
-        jnp.where(columns[None] == far_ids[:, None, None], (place + 2 * rows[:, None])[None], 0), axis=2
-    )
-    index = jnp.concatenate([right.reshape(-1), left.reshape(-1)])
-    index = jnp.where(index == 0, HELD, index - 1)
-    corner = lax.dynamic_slice(anchors, (0, first, 0), (3, UNIT, K))
-    planes = (corner[0] - 16 * (unit // 8) + 8 + 256) % 256
-    corners = jnp.concatenate([planes[None], corner[1:]], axis=0)
-    return index, corners.reshape(-1)
+    )(pattern, anchors, blocks, basis_x, basis_yz)
 
 
 def per_device(blocks, pattern, anchors, basis_x, basis_yz):
-    row = lax.axis_index("row")
-    col = lax.axis_index("col")
-    unit = 2 * ((row // 2) * 8 + place_of_col(col)) + row % 2
-    index, corners = tables(pattern, anchors, unit)
-    planes = jnp.concatenate([basis_x, jnp.zeros_like(basis_x)], axis=0).astype(jnp.float32)
-    cells = jnp.pad(basis_yz.reshape(B, 16, 16), ((0, 0), (0, 0), (0, 112))).reshape(B, 16 * 128)
-    square, grid = fused(index, corners, blocks.reshape(64, B, B), planes, cells)
+    square, grid = fused(pattern, anchors, blocks.reshape(64, B, B), basis_x, basis_yz)
     return square.reshape(32, 2, B, B).astype(jnp.float32), grid
 
 

time: 175 us -> 163 us (0.931)
  other arithmetic: 8.87 us -> 4.17 us
  Pallas kernels: 158 us -> 154 us
    pallas_call x1, Pallas kernels: 158 us -> 154 us  [fused(): pl.pallas_call(kernel, out_shape=[jax.ShapeDtypeStruct((64, B, B), jnp.bf...]
    unnamed x4 -> x5, local copies, waits for them, and re-layouts: 1.69 us -> 4.33 us
    slice x4 -> x0, local copies, waits for them, and re-layouts: 2.27 us -> none  [the longest x1 0.8 us: tables(): corners = jnp.concatenate([planes[None], corner[1:]], axis=0)]
where the time goes in v3:
time: 163 us
  Pallas kernels  154 us (94%)
  local copies, waits for them, and re-layouts  4.33 us (3%)
  other arithmetic  4.17 us (3%)
    pallas_call x1, Pallas kernels, fused(): pl.pallas_call(kernel, out_shape=[jax.ShapeDtypeStruct((64, B, B), jnp.bf...  154 us
    unnamed x5, local copies, waits for them, and re-layouts  4.33 us
    convert_element_type x1, other arithmetic, per_device(): return (square.reshape(32, 2, B, B).astype(jnp.float32), grid)  4.17 us

profile of v3, /device:TPU:1, one launch (start us, length us, event | category | flops | bytes accessed | tf_op | source)
XLA Modules:
  0.0 162.7 jit_solution(18338779014606007131)
XLA Ops:
  0.6 1.6 copy.7.pattern
  2.3 2.0 %copy.8.anchors = s32[3,512,16]{2,1,0:T(8,128)} copy(s32[3,512,16]{1,2,0:T(8,128)} %param.7) | data formatting | bytes 196608 | tf_op args[2]
  4.3 153.6 %square_and_tiles.1 = (bf16[64,128,128]{2,1,0:T(8,128)(2,1)}, f32[16,16,128]{2,1,0:T(8,128)}) custom-call(s32[512,16]{1,0:T(8,128)} %copy.7.pattern, s32[3,512,16]{2,1,0:T(8,128)} %copy.8.anchors, bf16[64,128,128]{2,1,0:T(8,128)(2,1)} %bitcast.4, bf16[16,128]{1,0:T(8,128)(2,1)} %basis_x.1, bf16[128,256]{1,0:T(8,128)(2,1)} %basis_yz.1), custom_call_target="tpu_custom_call" | custom-call | tf_op jit(solution)/shard_map/square_and_tiles/pallas_call | solution.py:373
  157.9 0.0 copy-start
  157.9 4.2 %convert.1 = f32[32,2,128,128]{3,2,1,0:T(8,128)} convert(bf16[32,2,128,128]{3,2,1,0:T(8,128)(2,1)} %bitcast.3) | non-fusion elementwise | flops 1048576 | bytes 6291456 | tf_op jit(solution)/shard_map/convert_element_type | solution.py:415
  162.0 0.0 copy-done
  162.0 0.7 copy.10
Async XLA Ops:
  157.9 4.2 %copy-start = (f32[16,16,128]{2,1,0:T(8,128)S(1)}, f32[16,16,128]{2,1,0:T(8,128)}, u32[]{:S(2)}) copy-start(f32[16,16,128]{2,1,0:T(8,128)} %get-tuple-element.9) | copy-start | bytes 393220

commit v4 on v3

--- a/solution.py
+++ b/solution.py
@@ -44,9 +44,9 @@
 def kernel(
     pattern, anchors, blocks, basis_x, basis_yz,
     square, grid,
-    held0, held1, held2, held3, held4, sums, density, halves, tiles, mid, low, high, own, below, above, total,
+    held0, held1, held2, held3, held4, sums, density, halves, tiles, mid, low, high, own, below, above, total, other_mid, other_low, other_high,
     rows_held, corners_held, planes, cells, drawn, index,
-    send_sem, recv_sem, fwd_send, fwd_recv, back_send, back_recv, table_sem,
+    send_sem, recv_sem, fwd_send, fwd_recv, back_send, back_recv, share_send, share_recv, table_sem,
 ):
     row = lax.axis_index("row")
     col = lax.axis_index("col")
@@ -75,19 +75,25 @@
         def _():
             signal(barrier, row_b, c)
 
-    @pl.loop(0, 24)
+    @pl.loop(0, 12)
     def _(v):
-        n = 8 * (row - 1) + v + 128
-        from_row, from_col = device_of(n // 2, lax.rem(n, 2))
-
-        @pl.when(jnp.logical_or(from_row != row, from_col != col))
-        def _():
-            signal(barrier, from_row, from_col)
+        from_share = 4 * (row - 1) + v
+
+        @pl.loop(0, 2)
+        def _(e):
+            from_row, from_col = device_of(from_share + SHARES, e)
+            sends_here = jnp.logical_or(v // 4 == 1, e == lax.rem(col, 2))
+
+            @pl.when(jnp.logical_and(sends_here, jnp.logical_or(from_row != row, from_col != col)))
+            def _():
+                signal(barrier, from_row, from_col)
 
     signal(barrier, *partner)
     place = lax.rem(share, 8)
     is_own = jnp.where(core == 0, place <= 4, place >= 3).astype(jnp.int32)
-    pl.semaphore_wait(barrier, 34 - is_own)
+    beside = jnp.logical_and(jnp.logical_or(up == row, down == row), lax.rem(col, 2) == core)
+    is_goal = jnp.logical_or(owner == row, beside).astype(jnp.int32)
+    pl.semaphore_wait(barrier, 27 - is_own - is_goal)
 
     plan = ((0, 1, 0, 1), (0, 0, 0, 0), (1, 0, -1, 1), (1, 1, 1, 0), (2, 0, 1, 0), (2, 1, -1, 1))
 
@@ -107,12 +113,11 @@
         is_here = jnp.logical_and(goal_row == row, goal_col == col)
         return src, dst, recv_sem.at[kind, col], away, is_here
 
-    for half in range(3):
-
+    def start_kind(kind):
         @pl.loop(0, 4)
         def _(w):
             v = lax.rem(w + col // 2, 4)
-            for item in plan[2 * half : 2 * half + 2]:
+            for item in plan[2 * kind : 2 * kind + 2]:
                 src, dst, sem, away, is_here = sends(v, *item)
 
                 @pl.when(is_here)
@@ -122,6 +127,9 @@
                 @pl.when(jnp.logical_not(is_here))
                 def _():
                     away.start()
+
+    start_kind(0)
+    start_kind(1)
 
     loads = (
         pltpu.make_async_copy(pattern, rows_held, table_sem.at[0]),
@@ -142,12 +150,13 @@
     @pl.loop(0, UNIT * K)
     def _(tile):
         for e in range(PAD):
-            tiles[tile * SPAN + e] = jnp.zeros((32, B), jnp.float32)
-            tiles[tile * SPAN + PAD + 16 + e] = jnp.zeros((32, B), jnp.float32)
+            tiles[tile * SPAN + e] = jnp.zeros((32, B), jnp.bfloat16)
+            tiles[tile * SPAN + PAD + 16 + e] = jnp.zeros((32, B), jnp.bfloat16)
 
     for load in loads:
         load.wait()
-    columns = rows_held[pl.ds(UNIT * unit, UNIT), :]
+    window = pltpu.roll(rows_held[...], lax.rem(2 * NBR + H - UNIT * unit, NBR), 1)[:, :B]
+    columns = jnp.transpose(window)[H : H + UNIT]
     own_row = lax.broadcasted_iota(jnp.int32, (UNIT, K), 0)
     own_slot = lax.broadcasted_iota(jnp.int32, (UNIT, K), 1)
     own_place = (own_slot // 2) * 8 + lax.rem(own_slot, 2) + 2 * own_row
@@ -159,7 +168,9 @@
         step = (0, -1, 1, 2, -2)[rank]
         far_unit = lax.rem(unit + step * (1 - 2 * core) + 128, 128)
         for cc in range(UNIT):
-            far = jnp.transpose(jnp.broadcast_to(rows_held[pl.ds(UNIT * far_unit + cc, 1), :], (K, K)))
+            lanes = [UNIT * (2 + sign * step) + cc for sign in (1, -1)]
+            far = jnp.where(core == 0, *[window[:, lane : lane + 1] for lane in lanes])
+            far = jnp.broadcast_to(far, (K, K))
             rights = []
             for i in range(UNIT):
                 fits = far == jnp.broadcast_to(columns[i : i + 1], (K, K))
@@ -173,7 +184,8 @@
             at = (rank * UNIT + cc) * UNIT
             drawn[at : at + UNIT, :] = jnp.where(wide < K, jnp.tile(right, (1, B // K)), left)
     for d in range(3):
-        corner = corners_held[d, pl.ds(UNIT * unit, UNIT), :]
+        corner = pltpu.roll(corners_held[d], lax.rem(NBR - UNIT * unit, NBR), 1)[:, :B]
+        corner = jnp.transpose(corner)[:UNIT]
         if d == 0:
             corner = lax.rem(corner - 16 * owner + 8 + 256, 256)
         at = CORNERS + d * UNIT
@@ -205,6 +217,9 @@
         def _(c):
             wait_for(f, c)
             forward(f, c).start()
+
+        if f == 0:
+            start_kind(2)
 
     def product(rank, i, pair):
         out = jnp.zeros((B, 2 * B), jnp.float32)
@@ -228,7 +243,7 @@
             def _(c):
                 forward(rank - 2, c).wait()
 
-        @pl.loop(0, UNIT * K // 2)
+        @pl.loop(0, UNIT * K // 2, unroll=4)
         def _(at):
             value = product(rank, at // (K // 2), lax.rem(at, K // 2))
             sums[at] = value if rank == 0 else sums[at] + value
@@ -240,19 +255,20 @@
     def goes_back(kind, c):
         src, dst, to_row = (
             (density.at[pl.ds(2 * UNIT * c, 2 * UNIT)], square.at[pl.ds(2 * UNIT * u_back, 2 * UNIT)], owner),
-            (mid.at[pl.ds(16 * c, 16)], own.at[u_back], owner),
-            (low.at[pl.ds(8 * c, 8)], above.at[u_back], down),
-            (high.at[pl.ds(8 * c, 8)], below.at[u_back], up),
+            (mid.at[pl.ds(16 * c, 16)], own.at[u_back // 2], owner),
+            (low.at[pl.ds(8 * c, 8)], above.at[u_back // 2], down),
+            (high.at[pl.ds(8 * c, 8)], below.at[u_back // 2], up),
         )[kind]
+        slot = u_back if kind == 0 else u_back // 2
         away = pltpu.make_async_remote_copy(
             src_ref=src,
             dst_ref=dst,
             send_sem=back_send.at[kind, c],
-            recv_sem=back_recv.at[kind, u_back],
+            recv_sem=back_recv.at[kind, slot],
             device_id=(to_row, c),
             device_id_type=MESH,
         )
-        return src, dst, back_recv.at[kind, u_back], away, jnp.logical_and(to_row == row, c == col)
+        return src, dst, back_recv.at[kind, slot], away, jnp.logical_and(to_row == row, c == col)
 
     def start_back(kind, c):
         src, dst, sem, away, is_here = goes_back(kind, c)
@@ -269,7 +285,7 @@
     def _(w):
         pair = lax.rem(w + col, COLS)
 
-        @pl.loop(0, UNIT)
+        @pl.loop(0, UNIT, unroll=4)
         def _(i):
             value = (sums[i * (K // 2) + pair] + product(4, i, pair)).astype(jnp.bfloat16)
             for e in range(2):
@@ -279,8 +295,7 @@
 
     @pl.loop(0, UNIT)
     def _(i):
-        @pl.loop(0, K // 2)
-        def _(pair):
+        for pair in range(K // 2):
             for e in range(2):
                 tile = 2 * pair + e
                 placed = pltpu.roll(planes[...], index[CORNERS + i, tile], 0).astype(jnp.bfloat16)
@@ -298,44 +313,80 @@
                 for e in range(4):
                     for f in range(2):
                         piece = values[e * 32 : (e + 1) * 32, f * 128 : (f + 1) * 128]
-                        tiles[(i * K + 4 * four + e) * SPAN + PAD + b + f] = pltpu.roll(piece, shifts[e], 1)
-
-    @pl.loop(0, COLS)
+                        tiles[(i * K + 4 * four + e) * SPAN + PAD + b + f] = pltpu.roll(piece, shifts[e], 1).astype(
+                            jnp.bfloat16
+                        )
+
+    def partial(eight):
+        def add_tile(tile, values):
+            off = 8 * eight - index[CORNERS + UNIT + tile // K, lax.rem(tile, K)]
+            inside = jnp.logical_and(off > -PAD, off < 16)
+            start = tile * SPAN + jnp.where(inside, off + PAD, 0)
+            return tuple(value + tiles[start + y].astype(jnp.float32) for y, value in enumerate(values))
+
+        zeros = tuple(jnp.zeros((32, B), jnp.float32) for _ in range(8))
+        values = lax.fori_loop(0, UNIT * K, add_tile, zeros, unroll=8)
+        pairs = [values[2 * y : 2 * y + 2] for y in range(4)]
+        mids = [value[8:24] for value in values]
+        lows = [jnp.concatenate([first[0:8], second[0:8]], axis=0) for first, second in pairs]
+        highs = [jnp.concatenate([first[24:32], second[24:32]], axis=0) for first, second in pairs]
+        return mids, lows, highs
+
+    def share_parts(kind, c):
+        ref, other = ((mid, other_mid), (low, other_low), (high, other_high))[kind]
+        size = 16 if kind == 0 else 8
+        return pltpu.make_async_remote_copy(
+            src_ref=ref.at[pl.ds(size * c, size)],
+            dst_ref=other.at[c // 2],
+            send_sem=share_send.at[kind, c // 2],
+            recv_sem=share_recv.at[kind, c // 2],
+            device_id=partner,
+            device_id_type=MESH,
+        )
+
+    @pl.loop(0, COLS // 2)
     def _(w):
-        c = lax.rem(w + col, COLS)
+        c = 2 * lax.rem(w + col // 2, COLS // 2) + 1 - core
 
         @pl.loop(0, 2)
         def _(h):
-            eight = 2 * c + h
-
-            def add_tile(tile, values):
-                off = 8 * eight - index[CORNERS + UNIT + tile // K, lax.rem(tile, K)]
-                inside = jnp.logical_and(off > -PAD, off < 16)
-                start = tile * SPAN + jnp.where(inside, off + PAD, 0)
-                return tuple(value + tiles[start + y] for y, value in enumerate(values))
-
-            values = lax.fori_loop(
-                0, UNIT * K, add_tile, tuple(jnp.zeros((32, B), jnp.float32) for _ in range(8)), unroll=2
-            )
-            for y in range(8):
-                mid[8 * eight + y] = values[y][8:24].astype(jnp.bfloat16)
-            for y in range(4):
-                first, second = values[2 * y], values[2 * y + 1]
-                low[4 * eight + y] = jnp.concatenate([first[0:8], second[0:8]], axis=0).astype(jnp.bfloat16)
-                high[4 * eight + y] = jnp.concatenate([first[24:32], second[24:32]], axis=0).astype(jnp.bfloat16)
+            for ref, values in zip((mid, low, high), partial(2 * c + h)):
+                for y, value in enumerate(values):
+                    ref[(2 * c + h) * len(values) + y] = value.astype(jnp.bfloat16)
+
+        for kind in range(3):
+            share_parts(kind, c).start()
+
+    @pl.loop(0, COLS // 2)
+    def _(w):
+        c = 2 * lax.rem(w + col // 2, COLS // 2) + core
+        for kind in range(3):
+            share_parts(kind, c).wait_recv()
+
+        @pl.loop(0, 2)
+        def _(h):
+            others = (other_mid, other_low, other_high)
+            for ref, other, values in zip((mid, low, high), others, partial(2 * c + h)):
+                for y, value in enumerate(values):
+                    value += other[c // 2, h * len(values) + y].astype(jnp.float32)
+                    ref[(2 * c + h) * len(values) + y] = value.astype(jnp.bfloat16)
 
         for kind in (1, 2, 3):
             start_back(kind, c)
 
     @pl.loop(0, 8)
     def _(v):
-        refs = (square.at[pl.ds(2 * UNIT * v, 2 * UNIT)], own.at[v], above.at[v], below.at[v])
-        for kind, ref in enumerate(refs):
-            pltpu.make_async_copy(ref, ref, back_recv.at[kind, v]).wait()
+        ref = square.at[pl.ds(2 * UNIT * v, 2 * UNIT)]
+        pltpu.make_async_copy(ref, ref, back_recv.at[0, v]).wait()
+
+    @pl.loop(0, 4)
+    def _(v):
+        for kind, ref in enumerate((own.at[v], above.at[v], below.at[v])):
+            pltpu.make_async_copy(ref, ref, back_recv.at[kind + 1, v]).wait()
 
     def added(ref, at):
         value = ref[0, at].astype(jnp.float32)
-        for v in range(1, 8):
+        for v in range(1, 4):
             value += ref[v, at].astype(jnp.float32)
         return value
 
@@ -359,14 +410,22 @@
             def _():
                 away.wait_send()
 
+    def end_back(kind, c):
+        away, is_here = goes_back(kind, c)[3:]
+
+        @pl.when(jnp.logical_not(is_here))
+        def _():
+            away.wait_send()
+
     @pl.loop(0, COLS)
     def _(c):
-        for kind in range(4):
-            away, is_here = goes_back(kind, c)[3:]
-
-            @pl.when(jnp.logical_not(is_here))
-            def _():
-                away.wait_send()
+        end_back(0, c)
+
+    @pl.loop(0, COLS // 2)
+    def _(w):
+        for kind in range(3):
+            share_parts(kind, 2 * w + 1 - core).wait_send()
+            end_back(kind + 1, 2 * w + core)
 
 
 def fused(pattern, anchors, blocks, basis_x, basis_yz):
@@ -383,16 +442,19 @@
             pltpu.VMEM((UNIT * K // 2, B, 2 * B), jnp.float32),
             pltpu.VMEM((HELD, B, B), jnp.bfloat16),
             pltpu.VMEM((K * 32, B), jnp.bfloat16),
-            pltpu.VMEM((UNIT * K * SPAN, 32, 128), jnp.float32),
+            pltpu.VMEM((UNIT * K * SPAN, 32, 128), jnp.bfloat16),
             pltpu.VMEM((128, 16, 128), jnp.bfloat16),
             pltpu.VMEM((64, 16, 128), jnp.bfloat16),
             pltpu.VMEM((64, 16, 128), jnp.bfloat16),
-            pltpu.VMEM((8, 16, 16, 128), jnp.bfloat16),
-            pltpu.VMEM((8, 8, 16, 128), jnp.bfloat16),
-            pltpu.VMEM((8, 8, 16, 128), jnp.bfloat16),
+            pltpu.VMEM((4, 16, 16, 128), jnp.bfloat16),
+            pltpu.VMEM((4, 8, 16, 128), jnp.bfloat16),
+            pltpu.VMEM((4, 8, 16, 128), jnp.bfloat16),
             pltpu.VMEM((256, 128), jnp.float32),
-            pltpu.VMEM((NBR, K), jnp.int32),
-            pltpu.VMEM((3, NBR, K), jnp.int32),
+            pltpu.VMEM((4, 16, 16, 128), jnp.bfloat16),
+            pltpu.VMEM((4, 8, 16, 128), jnp.bfloat16),
+            pltpu.VMEM((4, 8, 16, 128), jnp.bfloat16),
+            pltpu.VMEM((K, NBR), jnp.int32),
+            pltpu.VMEM((3, K, NBR), jnp.int32),
             pltpu.VMEM((32, B), jnp.float32),
             pltpu.VMEM((B, 16 * B), jnp.bfloat16),
             pltpu.VMEM((TABLE, B), jnp.int32),
@@ -403,6 +465,8 @@
             pltpu.SemaphoreType.DMA((2, COLS)),
             pltpu.SemaphoreType.DMA((4, COLS)),
             pltpu.SemaphoreType.DMA((4, 8)),
+            pltpu.SemaphoreType.DMA((3, 4)),
+            pltpu.SemaphoreType.DMA((3, 4)),
             pltpu.SemaphoreType.DMA((3,)),
         ],
         compiler_params=pltpu.CompilerParams(collective_id=0, has_side_effects=True, vmem_limit_bytes=60 << 20),
@@ -411,7 +475,7 @@
 
 
 def per_device(blocks, pattern, anchors, basis_x, basis_yz):
-    square, grid = fused(pattern, anchors, blocks.reshape(64, B, B), basis_x, basis_yz)
+    square, grid = fused(pattern.T, jnp.transpose(anchors, (0, 2, 1)), blocks.reshape(64, B, B), basis_x, basis_yz)
     return square.reshape(32, 2, B, B).astype(jnp.float32), grid
 
 

time: 163 us -> 124 us (0.76)
  Pallas kernels: 154 us -> 118 us
  local copies, waits for them, and re-layouts: 4.33 us -> 0.66 us
    pallas_call x1, Pallas kernels: 154 us -> 118 us  [fused(): pl.pallas_call(kernel, out_shape=[jax.ShapeDtypeStruct((64, B, B), jnp.bf...]
    unnamed x5 -> x3, local copies, waits for them, and re-layouts: 4.33 us -> 0.66 us
where the time goes in v4:
time: 124 us
  Pallas kernels  118 us (95%)
  other arithmetic  4.17 us (3%)
    pallas_call x1, Pallas kernels, fused(): pl.pallas_call(kernel, out_shape=[jax.ShapeDtypeStruct((64, B, B), jnp.bf...  118 us
    convert_element_type x1, other arithmetic, per_device(): return (square.reshape(32, 2, B, B).astype(jnp.float32), grid)  4.17 us

profile of v4, /device:TPU:1, one launch (start us, length us, event | category | flops | bytes accessed | tf_op | source)
XLA Modules:
  0.0 123.6 jit_solution(12062061293943812253)
XLA Ops:
  0.6 118.1 %square_and_tiles.1 = (bf16[64,128,128]{2,1,0:T(8,128)(2,1)}, f32[16,16,128]{2,1,0:T(8,128)}) custom-call(s32[16,512]{1,0:T(8,128)} %bitcast.8, s32[3,16,512]{2,1,0:T(8,128)} %bitcast.7, bf16[64,128,128]{2,1,0:T(8,128)(2,1)} %bitcast.6, bf16[16,128]{1,0:T(8,128)(2,1)} %basis_x.1, bf16[128,256]{1,0:T(8,128)(2,1)} %basis_yz.1), custom_call_target="tpu_custom_call" | custom-call | tf_op jit(solution)/shard_map/square_and_tiles/pallas_call | solution.py:432
  118.8 0.0 copy-start
  118.8 4.2 %convert.1 = f32[32,2,128,128]{3,2,1,0:T(8,128)} convert(bf16[32,2,128,128]{3,2,1,0:T(8,128)(2,1)} %bitcast.5) | non-fusion elementwise | flops 1048576 | bytes 6291456 | tf_op jit(solution)/shard_map/convert_element_type | solution.py:479
  122.9 0.0 copy-done
  122.9 0.7 copy.8
Async XLA Ops:
  118.8 4.2 %copy-start = (f32[16,16,128]{2,1,0:T(8,128)S(1)}, f32[16,16,128]{2,1,0:T(8,128)}, u32[]{:S(2)}) copy-start(f32[16,16,128]{2,1,0:T(8,128)} %get-tuple-element.9) | copy-start | bytes 393220

commit v5 on v4

--- a/solution.py
+++ b/solution.py
@@ -221,9 +221,9 @@
         if f == 0:
             start_kind(2)
 
-    def product(rank, i, pair):
+    def product(rank, i, pair, parts=(0, 2)):
         out = jnp.zeros((B, 2 * B), jnp.float32)
-        for kk in range(0, UNIT, 2):
+        for kk in parts:
             lefts = [held0[index[(rank * UNIT + kk + e) * UNIT + i, K]] for e in range(2)]
             rights = []
             for e in range(2):
@@ -283,11 +283,13 @@
 
     @pl.loop(0, COLS)
     def _(w):
-        pair = lax.rem(w + col, COLS)
-
-        @pl.loop(0, UNIT, unroll=4)
-        def _(i):
-            value = (sums[i * (K // 2) + pair] + product(4, i, pair)).astype(jnp.bfloat16)
+        pair = lax.rem(w + col + 1, COLS)
+
+        near, far = 2 * (1 - core), 2 * core
+        for j in range(UNIT):
+            i = far + j if j < 2 else near + j - 2
+            value = sums[i * (K // 2) + pair] + product(4, i, pair, (near, far) if j < 2 else (near,))
+            value = value.astype(jnp.bfloat16)
             for e in range(2):
                 density[2 * UNIT * pair + 2 * i + e] = value[:, e * B : (e + 1) * B]
 
@@ -325,7 +327,7 @@
             return tuple(value + tiles[start + y].astype(jnp.float32) for y, value in enumerate(values))
 
         zeros = tuple(jnp.zeros((32, B), jnp.float32) for _ in range(8))
-        values = lax.fori_loop(0, UNIT * K, add_tile, zeros, unroll=8)
+        values = lax.fori_loop(0, UNIT * K, add_tile, zeros, unroll=16)
         pairs = [values[2 * y : 2 * y + 2] for y in range(4)]
         mids = [value[8:24] for value in values]
         lows = [jnp.concatenate([first[0:8], second[0:8]], axis=0) for first, second in pairs]

time: 124 us -> 124 us (level)
  no operation moved by 1% of the time
where the time goes in v5:
time: 124 us; the launch traced here: 123 us
  Pallas kernels  118 us (95%)
  other arithmetic  4.17 us (3%)
    pallas_call x1, Pallas kernels, fused(): pl.pallas_call(kernel, out_shape=[jax.ShapeDtypeStruct((64, B, B), jnp.bf...  118 us
    convert_element_type x1, other arithmetic, per_device(): return (square.reshape(32, 2, B, B).astype(jnp.float32), grid)  4.17 us

profile of v5, /device:TPU:1, one launch (start us, length us, event | category | flops | bytes accessed | tf_op | source)
XLA Modules:
  0.0 123.5 jit_solution(6962996844501188037)
XLA Ops:
  0.6 118.0 %square_and_tiles.1 = (bf16[64,128,128]{2,1,0:T(8,128)(2,1)}, f32[16,16,128]{2,1,0:T(8,128)}) custom-call(s32[16,512]{1,0:T(8,128)} %bitcast.8, s32[3,16,512]{2,1,0:T(8,128)} %bitcast.7, bf16[64,128,128]{2,1,0:T(8,128)(2,1)} %bitcast.6, bf16[16,128]{1,0:T(8,128)(2,1)} %basis_x.1, bf16[128,256]{1,0:T(8,128)(2,1)} %basis_yz.1), custom_call_target="tpu_custom_call" | custom-call | tf_op jit(solution)/shard_map/square_and_tiles/pallas_call | solution.py:434
  118.6 0.0 copy-start
  118.6 4.2 %convert.1 = f32[32,2,128,128]{3,2,1,0:T(8,128)} convert(bf16[32,2,128,128]{3,2,1,0:T(8,128)(2,1)} %bitcast.5) | non-fusion elementwise | flops 1048576 | bytes 6291456 | tf_op jit(solution)/shard_map/convert_element_type | solution.py:481
  122.8 0.0 copy-done
  122.8 0.7 copy.8
Async XLA Ops:
  118.6 4.2 %copy-start = (f32[16,16,128]{2,1,0:T(8,128)S(1)}, f32[16,16,128]{2,1,0:T(8,128)}, u32[]{:S(2)}) copy-start(f32[16,16,128]{2,1,0:T(8,128)} %get-tuple-element.9) | copy-start | bytes 393220
